TPU v7x, 128 devices: a whole 4x4x4 slice. The times are simulated.
128 devices in a mesh: row: 32 (over y, z_hi, x), frame: 2 (over core), coil: 2 (over z_lo).
Axes of the slice: x: 4, y: 4, z: 4 (z_hi: 2, z_lo: 2; z = z_hi * 2 + z_lo), core: 2. Of those that a mesh axis runs over, the one named last changes fastest.
Arguments:
- factor_u: bfloat16 [2, 48, 1024, 1024], P(None, None, 'row'), may hold values from -4 to 4
- temporal_v: bfloat16 [2, 48], replicated, may hold values from -4 to 4
- sensitivity: bfloat16 [2, 16, 1024, 1024], P(None, 'coil', 'row'), may hold values from -4 to 4
- kspace_data: bfloat16 [2, 2, 16, 1024, 1024], P(None, 'frame', 'coil', 'row'), may hold values from -6 to 6
- sample_mask: int32 [2, 1024], P('frame'), may hold values 0 or 1
- tv_weight: float32 [1024, 1024], P('row'), may hold values from 0.5 to 2
Outputs:
- factor_grad: float32 [2, 48, 1024, 1024], P(None, None, 'row')
Inputs may be any that keep to these rules, and one draw needn't show every extreme that they name: `sample_mask`: 1 marks a sampled line.
All inputs are finite; a program needn't handle non-finite values. No bound on the sum of `sample_mask` on one device may be relied on, other than what follows from the above.
Results may differ from a plain program's by a relative error of at most 0.007.
Values may be sent and summed in bfloat16 or wider, within the bound.
A program may use at most 192 MiB of HBM per device.

v0:
```python
import math

import jax
import jax.numpy as jnp
import numpy as np
from jax import lax
from jax.experimental import pallas as pl
from jax.experimental.pallas import tpu as pltpu
from jax.sharding import PartitionSpec as P

N = 1024
ROWS = 32
RANK = 48
COILS = 8
GROUPS = 2
PER = COILS // GROUPS
DEVS = 32
TV_EPS = 0.25
TV_GAIN = 0.5
F32 = jnp.float32
BF16 = jnp.bfloat16


def fourier_tables():
    position = np.arange(N)
    angle = 2.0 * math.pi * ((position[:, None] * position[None, :]) % N) / N
    both = np.stack([np.cos(angle), np.sin(angle)]) / math.sqrt(N)
    return both.astype(jnp.bfloat16)


def swap_blocks(parts):
    lane = lax.broadcasted_iota(jnp.int32, parts[0].shape, 1)
    even = (lane // 32) % 2 == 0
    low = lane < 64
    a = list(parts)
    for x, y in ((0, 1), (2, 3)):
        first = jnp.where(even, a[x], pltpu.roll(a[y], 32, 1))
        second = jnp.where(even, pltpu.roll(a[x], 96, 1), a[y])
        a[x], a[y] = first, second
    for x, y in ((0, 2), (1, 3)):
        first = jnp.where(low, a[x], pltpu.roll(a[y], 64, 1))
        second = jnp.where(low, pltpu.roll(a[x], 64, 1), a[y])
        a[x], a[y] = first, second
    return a


def dot(a, b):
    return jnp.dot(a, b, preferred_element_type=F32)


def main_kernel(
    v_ref, mask_ref, u_hbm, s_hbm, d_hbm, w_hbm, tab_hbm, out_ref,
    u, s, d, w, tab, f, a, dt, mcol, x, land, mis, b, r, lmat, acc, halo_s, halo_r, part_s, part_r, comb, tvg,
    u_sem, in_sem, halo_send, halo_recv, x_send, x_recv, b_send, b_recv, p_send, p_recv, c_send, c_recv,
):
    row = lax.axis_index("row")
    frame = lax.axis_index("frame")
    coil = lax.axis_index("coil")
    my_y = row // 8

    u_copies = []
    for q in range(4):
        part = (q // 2, slice(None), pl.ds((q % 2) * 16, 16))
        u_copies.append(pltpu.make_async_copy(u_hbm.at[part], u.at[part], u_sem.at[q]))
    for copy in u_copies:
        copy.start()
    in_copies = [
        pltpu.make_async_copy(src, dst, in_sem.at[q])
        for q, (src, dst) in enumerate(((s_hbm, s), (tab_hbm, tab), (w_hbm, w), (d_hbm, d)))
    ]
    for copy in in_copies:
        copy.start()

    barrier = pltpu.get_barrier_semaphore()

    def greet(i, carry):
        @pl.when(i != row)
        def _():
            pl.semaphore_signal(barrier, inc=1, device_id={"row": i}, device_id_type=pl.DeviceIdType.MESH)
        return carry

    lax.fori_loop(0, DEVS, greet, 0)
    pl.semaphore_signal(barrier, inc=1, device_id={"coil": 1 - coil}, device_id_type=pl.DeviceIdType.MESH)
    pl.semaphore_signal(barrier, inc=1, device_id={"frame": 1 - frame}, device_id_type=pl.DeviceIdType.MESH)

    for q in range(4):
        u_copies[q].wait()
        p, top = q // 2, (q % 2) * 16
        for half in range(2):
            total = jnp.zeros((16, 512), F32)
            for k in range(RANK):
                total += v_ref[frame, k] * u[p, k, top:top + 16, half * 512:(half + 1) * 512].astype(F32)
            f[p, top:top + 16, half * 512:(half + 1) * 512] = total

    in_copies[0].wait()
    in_copies[1].wait()
    in_copies[2].wait()
    halo_s[...] = jnp.zeros_like(halo_s)
    for p in range(2):
        halo_s[0, p:p + 1, :] = f[p, 0:1, :]
        halo_s[1, p:p + 1, :] = f[p, 31:32, :]
    halo_s[1, 2:3, :] = w[31:32, :]

    def coil_images(c, carry):
        sr = s[0, c].astype(F32)
        si = s[1, c].astype(F32)
        fr, fi = f[0], f[1]
        at = pl.multiple_of((c % PER) * 32, 32)
        a[c // PER, pl.ds(at, 32), :] = (sr * fr - si * fi).astype(BF16)
        a[c // PER, pl.ds(128 + at, 32), :] = (sr * fi + si * fr).astype(BF16)
        return carry

    lax.fori_loop(0, COILS, coil_images, 0)

    pl.semaphore_wait(barrier, DEVS + 1)

    up = pltpu.make_async_remote_copy(
        halo_s.at[0], halo_r.at[1], halo_send.at[0], halo_recv.at[1],
        device_id={"row": (row + DEVS - 1) % DEVS}, device_id_type=pl.DeviceIdType.MESH)
    down = pltpu.make_async_remote_copy(
        halo_s.at[1], halo_r.at[0], halo_send.at[1], halo_recv.at[0],
        device_id={"row": (row + 1) % DEVS}, device_id_type=pl.DeviceIdType.MESH)
    up.start()
    down.start()

    def send_eight(src, dst, send_sem, recv_sem, g, jj):
        for k in range(8):
            to = jj * 8 + k
            rows = pl.ds(pl.multiple_of(to * 32, 32), 32)
            mine = pl.ds(pl.multiple_of(row * 32, 32), 32)

            @pl.when(to != row)
            def _():
                pltpu.make_async_remote_copy(
                    src.at[g, rows], dst.at[g, mine], send_sem.at[g], recv_sem.at[g],
                    device_id={"row": to}, device_id_type=pl.DeviceIdType.MESH).start()

            @pl.when(to == row)
            def _():
                dst[g, mine, :] = src[g, mine, :]

    def wait_all(ref, sem, g):
        view = ref.at[g, pl.ds(0, N - 32)]
        pltpu.make_async_copy(view, view, sem.at[g]).wait()

    def forward_x(q, carry):
        g, step = q // 4, q % 4
        jj = (my_y + step) % 4
        cols = pl.ds(pl.multiple_of(jj * 256, 256), 256)
        lhs = a[g]
        c_part = dot(lhs, tab[0, :, cols])
        s_part = dot(lhs, tab[1, :, cols])
        both = (c_part[:128] + s_part[128:], c_part[128:] - s_part[:128])
        for p in range(2):
            for h in range(2):
                w4 = swap_blocks([both[p][c * 32:(c + 1) * 32, h * 128:(h + 1) * 128] for c in range(4)])
                for i in range(4):
                    at = pl.multiple_of((jj * 8 + h * 4 + i) * 32, 32)
                    x[g, pl.ds(at, 32), p * 128:(p + 1) * 128] = w4[i].astype(BF16)
        send_eight(x, land, x_send, x_recv, g, jj)
        return carry

    lax.fori_loop(0, 8, forward_x, 0)

    in_copies[3].wait()
    mask_rows = jnp.broadcast_to(mask_ref[...].astype(F32), (128, N))
    mcol[...] = mask_rows.T

    def turn(q, carry):
        g, p = q // 2, q % 2
        block = d[p, 0, pl.ds(g * PER, PER)].reshape(128, N).astype(F32)
        lanes = pl.ds(pl.multiple_of(p * 128, 128), 128)
        dt[g, :, lanes] = block.T.astype(BF16)
        return carry

    lax.fori_loop(0, 4, turn, 0)

    up.wait()
    down.wait()
    lane = lax.broadcasted_iota(jnp.int32, (ROWS, N), 1)
    line = lax.broadcasted_iota(jnp.int32, (ROWS, N), 0)
    last_col = lane == N - 1
    last_line = line == ROWS - 1
    across, downs = [], []
    for p in range(2):
        cur = f[p]
        across.append(jnp.where(last_col, 0.0, pltpu.roll(cur, N - 1, 1) - cur))
        below = jnp.where(last_line, halo_r[1, p:p + 1, :], pltpu.roll(cur, ROWS - 1, 0))
        downs.append(jnp.where(last_line & (row == DEVS - 1), 0.0, below - cur))
    scale = w[...] / jnp.sqrt(across[0] * across[0] + across[1] * across[1]
                              + downs[0] * downs[0] + downs[1] * downs[1] + TV_EPS)
    above = halo_r[0]
    top_across = jnp.where(lax.broadcasted_iota(jnp.int32, (8, N), 1) == N - 1, 0.0, pltpu.roll(above, N - 1, 1) - above)
    top_down = [f[p, 0:1, :] - above[p:p + 1] for p in range(2)]
    top_scale = above[2:3] / jnp.sqrt(top_across[0:1] * top_across[0:1] + top_across[1:2] * top_across[1:2]
                                      + top_down[0] * top_down[0] + top_down[1] * top_down[1] + TV_EPS)
    for p in range(2):
        fa = scale * across[p]
        fd = scale * downs[p]
        top = jnp.where(row == 0, 0.0, top_scale * top_down[p])
        left = jnp.where(lane == 0, 0.0, pltpu.roll(fa, 1, 1))
        over = jnp.where(line == 0, top, pltpu.roll(fd, 1, 0))
        tvg[p] = TV_GAIN * ((left - fa) + (over - fd))

    def middle(g, carry):
        wait_all(land, x_recv, g)

        def residual(kt, inner):
            rows = pl.ds(pl.multiple_of(kt * 256, 256), 256)
            c_part = dot(tab[0, rows, :], land[g])
            s_part = dot(tab[1, rows, :], land[g])
            keep = mcol[rows, :]
            real = c_part[:, :128] + s_part[:, 128:] - dt[g, rows, :128].astype(F32)
            imag = c_part[:, 128:] - s_part[:, :128] - dt[g, rows, 128:].astype(F32)
            mis[rows, :128] = (keep * real).astype(BF16)
            mis[rows, 128:] = (keep * imag).astype(BF16)
            return inner

        lax.fori_loop(0, 4, residual, 0)

        def back(step, inner):
            jj = (my_y + step) % 4
            rows = pl.ds(pl.multiple_of(jj * 256, 256), 256)
            c_part = dot(tab[0, rows, :], mis[...])
            s_part = dot(tab[1, rows, :], mis[...])
            b[g, rows, :128] = (c_part[:, :128] - s_part[:, 128:]).astype(BF16)
            b[g, rows, 128:] = (c_part[:, 128:] + s_part[:, :128]).astype(BF16)
            send_eight(b, r, b_send, b_recv, g, jj)
            return inner

        lax.fori_loop(0, 4, back, 0)
        return carry

    lax.fori_loop(0, GROUPS, middle, 0)

    for g in range(GROUPS):
        wait_all(r, b_recv, g)

        def gather(j, carry):
            lanes = pl.ds(pl.multiple_of(j * 128, 128), 128)
            for p in range(2):
                got = swap_blocks([
                    r[g, pl.ds(pl.multiple_of((4 * j + i) * 32, 32), 32), p * 128:(p + 1) * 128].astype(F32)
                    for i in range(4)])
                for c in range(4):
                    lmat[p * 128 + c * 32:p * 128 + (c + 1) * 32, lanes] = got[c].astype(BF16)
            return carry

        lax.fori_loop(0, 8, gather, 0)

        def inverse_x(xt, carry):
            cols = pl.ds(pl.multiple_of(xt * 256, 256), 256)
            lhs = lmat[...]
            c_part = dot(lhs, tab[0, :, cols])
            s_part = dot(lhs, tab[1, :, cols])
            real = c_part[:128] - s_part[128:]
            imag = c_part[128:] + s_part[:128]
            gr = jnp.zeros((32, 256), F32)
            gi = jnp.zeros((32, 256), F32)
            for c in range(PER):
                sr = s[0, g * PER + c, :, cols].astype(F32)
                si = s[1, g * PER + c, :, cols].astype(F32)
                br = real[c * 32:(c + 1) * 32]
                bi = imag[c * 32:(c + 1) * 32]
                gr += sr * br + si * bi
                gi += sr * bi - si * br
            if g == 0:
                acc[0, :, cols] = gr
                acc[1, :, cols] = gi
            else:
                part_s[xt, 0] = (acc[0, :, cols] + gr).astype(BF16)
                part_s[xt, 1] = (acc[1, :, cols] + gi).astype(BF16)
                pltpu.make_async_remote_copy(
                    part_s.at[xt], part_r.at[xt], p_send.at[xt], p_recv.at[xt],
                    device_id={"coil": 1 - coil}, device_id_type=pl.DeviceIdType.MESH).start()
            return carry

        lax.fori_loop(0, 4, inverse_x, 0)

    def finish(xt, carry):
        pltpu.make_async_copy(part_r.at[xt], part_r.at[xt], p_recv.at[xt]).wait()
        cols = pl.ds(pl.multiple_of(xt * 256, 256), 256)
        for p in range(2):
            whole = part_s[xt, p].astype(F32) + part_r[xt, p].astype(F32) + tvg[p, :, cols]
            comb[frame, xt, p] = whole
        pltpu.make_async_remote_copy(
            comb.at[frame, xt], comb.at[frame, xt], c_send.at[xt], c_recv.at[xt],
            device_id={"frame": 1 - frame}, device_id_type=pl.DeviceIdType.MESH).start()
        return carry

    lax.fori_loop(0, 4, finish, 0)
    for xt in range(4):
        pltpu.make_async_copy(comb.at[1 - frame, xt], comb.at[1 - frame, xt], c_recv.at[xt]).wait()
        pltpu.make_async_copy(comb.at[frame, xt], comb.at[frame, xt], c_send.at[xt]).wait()
        pltpu.make_async_copy(part_s.at[xt], part_s.at[xt], p_send.at[xt]).wait()
        for t in range(2):
            for p in range(2):
                out_ref[t, p, :, xt * 256:(xt + 1) * 256] = comb[t, xt, p]
    for g in range(GROUPS):
        wait_all(x, x_send, g)
        wait_all(b, b_send, g)


def outer_kernel(v_ref, g_ref, out_ref):
    block = pl.program_id(1)
    first = g_ref[0, 0]
    second = g_ref[1, 0]
    for k in range(out_ref.shape[1]):
        at = block * out_ref.shape[1] + k
        out_ref[0, k] = v_ref[0, at] * first + v_ref[1, at] * second


def shards(factor_u, temporal_v, sensitivity, kspace_data, sample_mask, tv_weight):
    table = jnp.asarray(fourier_tables())
    v = temporal_v.astype(F32)
    anywhere = pl.BlockSpec(memory_space=pl.ANY)
    dma = pltpu.SemaphoreType.DMA
    combined = pl.pallas_call(
        main_kernel,
        out_shape=jax.ShapeDtypeStruct((2, 2, ROWS, N), F32),
        in_specs=[
            pl.BlockSpec(memory_space=pltpu.SMEM), pl.BlockSpec(memory_space=pltpu.VMEM),
            anywhere, anywhere, anywhere, anywhere, anywhere,
        ],
        out_specs=pl.BlockSpec(memory_space=pltpu.VMEM),
        scratch_shapes=[
            pltpu.VMEM((2, RANK, ROWS, N), BF16),
            pltpu.VMEM((2, COILS, ROWS, N), BF16),
            pltpu.VMEM((2, 1, COILS, ROWS, N), BF16),
            pltpu.VMEM((ROWS, N), F32),
            pltpu.VMEM((2, N, N), BF16),
            pltpu.VMEM((2, ROWS, N), F32),
            pltpu.VMEM((GROUPS, 256, N), BF16),
            pltpu.VMEM((GROUPS, N, 256), BF16),
            pltpu.VMEM((N, 128), F32),
            pltpu.VMEM((GROUPS, N, 256), BF16),
            pltpu.VMEM((GROUPS, N, 256), BF16),
            pltpu.VMEM((N, 256), BF16),
            pltpu.VMEM((GROUPS, N, 256), BF16),
            pltpu.VMEM((GROUPS, N, 256), BF16),
            pltpu.VMEM((256, N), BF16),
            pltpu.VMEM((2, ROWS, N), F32),
            pltpu.VMEM((2, 8, N), F32),
            pltpu.VMEM((2, 8, N), F32),
            pltpu.VMEM((4, 2, ROWS, 256), BF16),
            pltpu.VMEM((4, 2, ROWS, 256), BF16),
            pltpu.VMEM((2, 4, 2, ROWS, 256), F32),
            pltpu.VMEM((2, ROWS, N), F32),
            dma((4,)), dma((4,)), dma((2,)), dma((2,)),
            dma((GROUPS,)), dma((GROUPS,)), dma((GROUPS,)), dma((GROUPS,)),
            dma((4,)), dma((4,)), dma((4,)), dma((4,)),
        ],
        compiler_params=pltpu.CompilerParams(
            collective_id=0, has_side_effects=True, vmem_limit_bytes=48 * 1024 * 1024
        ),
        cost_estimate=pl.CostEstimate(flops=9 * 10**9, bytes_accessed=14 * 10**6, transcendentals=40000),
        name="frame_gradient",
    )(v, sample_mask, factor_u, sensitivity, kspace_data, tv_weight, table)
    step = 12
    return pl.pallas_call(
        outer_kernel,
        out_shape=jax.ShapeDtypeStruct((2, RANK, ROWS, N), F32),
        grid=(2, RANK // step),
        in_specs=[
            pl.BlockSpec(memory_space=pltpu.SMEM),
            pl.BlockSpec((2, 1, ROWS, N), lambda p, k: (0, p, 0, 0)),
        ],
        out_specs=pl.BlockSpec((1, step, ROWS, N), lambda p, k: (p, k, 0, 0)),
        compiler_params=pltpu.CompilerParams(vmem_limit_bytes=24 * 1024 * 1024),
        cost_estimate=pl.CostEstimate(flops=10**7, bytes_accessed=13 * 10**6, transcendentals=0),
        name="spread_over_rank",
    )(v, combined)


def solution(mesh):
    return jax.shard_map(
        shards,
        mesh=mesh,
        in_specs=(
            P(None, None, "row", None),
            P(),
            P(None, "coil", "row", None),
            P(None, "frame", "coil", "row", None),
            P("frame", None),
            P("row", None),
        ),
        out_specs=P(None, None, "row", None),
        check_vma=False,
    )
```

profile of v0, /device:TPU:1, one launch (start us, length us, event | category | flops | bytes accessed | tf_op | source)
XLA Modules:
  0.0 58.9 jit_solution(9616829060684779249)
XLA Ops:
  0.0 0.7 %convert_element_type.3.v_ref = f32[2,48]{1,0:T(2,128)S(1)} convert(bf16[2,48]{1,0:T(2,128)(2,1)} %param.8) | non-fusion elementwise | flops 96 | bytes 576 | tf_op jit(solution)/shard_map/convert_element_type | solution.py:315
  0.7 0.0 copy-start
  0.7 1.2 %copy-done = bf16[2,8,32,1024]{3,2,1,0:T(8,128)(2,1)S(1)} copy-done((bf16[2,8,32,1024]{3,2,1,0:T(8,128)(2,1)S(1)}, bf16[2,8,32,1024]{3,2,1,0:T(8,128)(2,1)}, u32[]{:S(2)}) %copy-start) | copy-done | bytes 1048600
  1.9 0.0 copy-start.1
  1.9 1.2 %copy-done.1 = bf16[2,1,8,32,1024]{4,3,2,1,0:T(8,128)(2,1)S(1)} copy-done((bf16[2,1,8,32,1024]{4,3,2,1,0:T(8,128)(2,1)S(1)}, bf16[2,1,8,32,1024]{4,3,2,1,0:T(8,128)(2,1)}, u32[]{:S(2)}) %copy-start.1) | copy-done | bytes 1048600
  3.1 0.0 copy-start.2
  3.1 0.9 %copy-done.2 = f32[32,1024]{1,0:T(8,128)S(1)} copy-done((f32[32,1024]{1,0:T(8,128)S(1)}, f32[32,1024]{1,0:T(8,128)}, u32[]{:S(2)}) %copy-start.2) | copy-done | bytes 131096
  4.0 0.0 copy-start.3
  4.0 0.7 %copy-done.3 = s32[1,1024]{1,0:T(1,128)S(1)} copy-done((s32[1,1024]{1,0:T(1,128)S(1)}, s32[1,1024]{1,0:T(1,128)}, u32[]{:S(2)}) %copy-start.3) | copy-done | bytes 4120
  4.7 47.8 %frame_gradient.1.g_ref = f32[2,2,32,1024]{3,2,1,0:T(8,128)S(1)} custom-call(f32[2,48]{1,0:T(2,128)S(1)} %convert_element_type.3.v_ref, s32[1,1024]{1,0:T(1,128)S(1)} %copy-done.3, bf16[2,48,32,1024]{3,2,1,0:T(8,128)(2,1)} %u_hbm.1, bf16[2,8,32,1024]{3,2,1,0:T(8,128)(2,1)S(1)} %copy-done, bf16[2,1,8,32,1024]{4,3,2,1,0:T(8,128)(2,1)S(1)} %copy-done.1, ...), custom_call_target="tpu_custom_call" | custom-call | flops 8999999488 | bytes 14000000 | tf_op jit(solution)/shard_map/frame_gradient/pallas_call | solution.py:318
  52.5 6.5 %spread_over_rank.1 = f32[2,48,32,1024]{3,2,1,0:T(8,128)} custom-call(f32[2,48]{1,0:T(2,128)S(1)} %convert_element_type.3.v_ref, f32[2,2,32,1024]{3,2,1,0:T(8,128)S(1)} %frame_gradient.1.g_ref), custom_call_target="tpu_custom_call" | custom-call | flops 10000000 | bytes 13000000 | tf_op jit(solution)/shard_map/spread_over_rank/pallas_call | solution.py:360
Async XLA Ops:
  0.7 1.2 %copy-start = (bf16[2,8,32,1024]{3,2,1,0:T(8,128)(2,1)S(1)}, bf16[2,8,32,1024]{3,2,1,0:T(8,128)(2,1)}, u32[]{:S(2)}) copy-start(bf16[2,8,32,1024]{3,2,1,0:T(8,128)(2,1)} %s_hbm.1) | copy-start | bytes 3145732
  1.9 1.2 %copy-start.1 = (bf16[2,1,8,32,1024]{4,3,2,1,0:T(8,128)(2,1)S(1)}, bf16[2,1,8,32,1024]{4,3,2,1,0:T(8,128)(2,1)}, u32[]{:S(2)}) copy-start(bf16[2,1,8,32,1024]{4,3,2,1,0:T(8,128)(2,1)} %d_hbm.1) | copy-start | bytes 3145732
  3.1 0.9 %copy-start.2 = (f32[32,1024]{1,0:T(8,128)S(1)}, f32[32,1024]{1,0:T(8,128)}, u32[]{:S(2)}) copy-start(f32[32,1024]{1,0:T(8,128)} %w_hbm.1) | copy-start | bytes 393220
  4.0 0.7 %copy-start.3 = (s32[1,1024]{1,0:T(1,128)S(1)}, s32[1,1024]{1,0:T(1,128)}, u32[]{:S(2)}) copy-start(s32[1,1024]{1,0:T(1,128)} %mask_ref.1) | copy-start | bytes 12292
where the time goes:
time: 59.2 us; the launch traced here: 58.9 us
  Pallas kernels  54.2 us (92%)
  local copies, waits for them, and re-layouts  4.04 us (7%)
  other arithmetic  0.66 us (1%)
    pallas_call x1, Pallas kernels, shards(): pl.pallas_call(main_kernel, out_shape=jax.ShapeDtypeStruct((2, 2, ROWS, N...  47.8 us
    pallas_call x1, Pallas kernels, shards(): pl.pallas_call(outer_kernel, out_shape=jax.ShapeDtypeStruct((2, RANK, ROW...  6.46 us
    unnamed x8, local copies, waits for them, and re-layouts  4.04 us

commit v1 on v0

--- a/solution.py
+++ b/solution.py
@@ -15,17 +15,30 @@
 GROUPS = 2
 PER = COILS // GROUPS
 DEVS = 32
+VMEM_LIMIT = 64 * 1024 * 1024 - 640 * 1024
 TV_EPS = 0.25
 TV_GAIN = 0.5
 F32 = jnp.float32
 BF16 = jnp.bfloat16
 
 
-def fourier_tables():
-    position = np.arange(N)
-    angle = 2.0 * math.pi * ((position[:, None] * position[None, :]) % N) / N
-    both = np.stack([np.cos(angle), np.sin(angle)]) / math.sqrt(N)
-    return both.astype(jnp.bfloat16)
+def angle_pair(product):
+    angle = 2.0 * math.pi * (product % N) / N
+    return np.cos(angle) / math.sqrt(N), np.sin(angle) / math.sqrt(N)
+
+
+def x_table():
+    at = np.arange(N)
+    return np.concatenate(angle_pair(at[:, None] * at[None, :])).astype(jnp.bfloat16)
+
+
+def y_tables():
+    quarter = np.arange(N // 4)
+    sides = []
+    for q in range(4):
+        cosine, sine = angle_pair((4 * quarter[:, None] + q) * quarter[None, :])
+        sides.append((np.concatenate([cosine, sine], axis=1), np.concatenate([cosine.T, sine.T], axis=1)))
+    return np.stack([np.stack([side[k] for side in sides]) for k in range(2)]).astype(jnp.bfloat16)
 
 
 def swap_blocks(parts):
@@ -49,8 +62,8 @@
 
 
 def main_kernel(
-    v_ref, mask_ref, u_hbm, s_hbm, d_hbm, w_hbm, tab_hbm, out_ref,
-    u, s, d, w, tab, f, a, dt, mcol, x, land, mis, b, r, lmat, acc, halo_s, halo_r, part_s, part_r, comb, tvg,
+    v_hbm, mask_hbm, u_hbm, s_hbm, d_hbm, w_hbm, xtab_hbm, ytab_hbm, out_ref,
+    u, s, d, w, xtab, ytab, mask_ref, v_ref, vcol, f, a, dt, dturn, mcol, mturn, x, land, uq, mis, bq, b, r, lmat, acc, halo_s, halo_r, part_s, part_r, comb, tvg,
     u_sem, in_sem, halo_send, halo_recv, x_send, x_recv, b_send, b_recv, p_send, p_recv, c_send, c_recv,
 ):
     row = lax.axis_index("row")
@@ -58,17 +71,17 @@
     coil = lax.axis_index("coil")
     my_y = row // 8
 
+    in_copies = []
+    names = ((v_hbm, v_ref), (s_hbm, s), (w_hbm, w), (xtab_hbm, xtab), (mask_hbm, mask_ref), (d_hbm, d), (ytab_hbm, ytab))
+    for q, (src, dst) in enumerate(names):
+        in_copies.append(pltpu.make_async_copy(src, dst, in_sem.at[q]))
+    v_in, s_in, w_in, xtab_in, mask_in, d_in, ytab_in = in_copies
     u_copies = []
     for q in range(4):
         part = (q // 2, slice(None), pl.ds((q % 2) * 16, 16))
         u_copies.append(pltpu.make_async_copy(u_hbm.at[part], u.at[part], u_sem.at[q]))
-    for copy in u_copies:
-        copy.start()
-    in_copies = [
-        pltpu.make_async_copy(src, dst, in_sem.at[q])
-        for q, (src, dst) in enumerate(((s_hbm, s), (tab_hbm, tab), (w_hbm, w), (d_hbm, d)))
-    ]
-    for copy in in_copies:
+    v_in.start()
+    for copy in u_copies + in_copies[1:]:
         copy.start()
 
     barrier = pltpu.get_barrier_semaphore()
@@ -83,18 +96,19 @@
     pl.semaphore_signal(barrier, inc=1, device_id={"coil": 1 - coil}, device_id_type=pl.DeviceIdType.MESH)
     pl.semaphore_signal(barrier, inc=1, device_id={"frame": 1 - frame}, device_id_type=pl.DeviceIdType.MESH)
 
+    v_in.wait()
+    spread_column(v_ref[...].astype(F32), frame, vcol)
     for q in range(4):
         u_copies[q].wait()
         p, top = q // 2, (q % 2) * 16
         for half in range(2):
             total = jnp.zeros((16, 512), F32)
             for k in range(RANK):
-                total += v_ref[frame, k] * u[p, k, top:top + 16, half * 512:(half + 1) * 512].astype(F32)
+                total += vcol[k:k + 1, :] * u[p, k, top:top + 16, half * 512:(half + 1) * 512].astype(F32)
             f[p, top:top + 16, half * 512:(half + 1) * 512] = total
 
-    in_copies[0].wait()
-    in_copies[1].wait()
-    in_copies[2].wait()
+    s_in.wait()
+    w_in.wait()
     halo_s[...] = jnp.zeros_like(halo_s)
     for p in range(2):
         halo_s[0, p:p + 1, :] = f[p, 0:1, :]
@@ -106,11 +120,16 @@
         si = s[1, c].astype(F32)
         fr, fi = f[0], f[1]
         at = pl.multiple_of((c % PER) * 32, 32)
-        a[c // PER, pl.ds(at, 32), :] = (sr * fr - si * fi).astype(BF16)
-        a[c // PER, pl.ds(128 + at, 32), :] = (sr * fi + si * fr).astype(BF16)
+        real = (sr * fr - si * fi).astype(BF16)
+        imag = (sr * fi + si * fr).astype(BF16)
+        a[c // PER, pl.ds(at, 32), :N] = real
+        a[c // PER, pl.ds(at, 32), N:] = imag
+        a[c // PER, pl.ds(128 + at, 32), :N] = imag
+        a[c // PER, pl.ds(128 + at, 32), N:] = -real
         return carry
 
     lax.fori_loop(0, COILS, coil_images, 0)
+    xtab_in.wait()
 
     pl.semaphore_wait(barrier, DEVS + 1)
 
@@ -123,21 +142,19 @@
     up.start()
     down.start()
 
-    def send_eight(src, dst, send_sem, recv_sem, g, jj):
-        for k in range(8):
-            to = jj * 8 + k
-            rows = pl.ds(pl.multiple_of(to * 32, 32), 32)
-            mine = pl.ds(pl.multiple_of(row * 32, 32), 32)
-
-            @pl.when(to != row)
-            def _():
-                pltpu.make_async_remote_copy(
-                    src.at[g, rows], dst.at[g, mine], send_sem.at[g], recv_sem.at[g],
-                    device_id={"row": to}, device_id_type=pl.DeviceIdType.MESH).start()
-
-            @pl.when(to == row)
-            def _():
-                dst[g, mine, :] = src[g, mine, :]
+    def send_rows(src, dst, send_sem, recv_sem, g, to):
+        rows = pl.ds(pl.multiple_of(to * 32, 32), 32)
+        mine = pl.ds(pl.multiple_of(row * 32, 32), 32)
+
+        @pl.when(to != row)
+        def _():
+            pltpu.make_async_remote_copy(
+                src.at[g, rows], dst.at[g, mine], send_sem.at[g], recv_sem.at[g],
+                device_id={"row": to}, device_id_type=pl.DeviceIdType.MESH).start()
+
+        @pl.when(to == row)
+        def _():
+            dst[g, mine, :] = src[g, mine, :]
 
     def wait_all(ref, sem, g):
         view = ref.at[g, pl.ds(0, N - 32)]
@@ -147,33 +164,35 @@
         g, step = q // 4, q % 4
         jj = (my_y + step) % 4
         cols = pl.ds(pl.multiple_of(jj * 256, 256), 256)
-        lhs = a[g]
-        c_part = dot(lhs, tab[0, :, cols])
-        s_part = dot(lhs, tab[1, :, cols])
-        both = (c_part[:128] + s_part[128:], c_part[128:] - s_part[:128])
+        both = dot(a[g], xtab[:, cols])
         for p in range(2):
             for h in range(2):
-                w4 = swap_blocks([both[p][c * 32:(c + 1) * 32, h * 128:(h + 1) * 128] for c in range(4)])
+                w4 = swap_blocks([both[p * 128 + c * 32:p * 128 + (c + 1) * 32, h * 128:(h + 1) * 128] for c in range(4)])
                 for i in range(4):
                     at = pl.multiple_of((jj * 8 + h * 4 + i) * 32, 32)
                     x[g, pl.ds(at, 32), p * 128:(p + 1) * 128] = w4[i].astype(BF16)
-        send_eight(x, land, x_send, x_recv, g, jj)
+        for k in range(8):
+            send_rows(x, land, x_send, x_recv, g, jj * 8 + k)
         return carry
 
     lax.fori_loop(0, 8, forward_x, 0)
 
-    in_copies[3].wait()
-    mask_rows = jnp.broadcast_to(mask_ref[...].astype(F32), (128, N))
-    mcol[...] = mask_rows.T
-
-    def turn(q, carry):
-        g, p = q // 2, q % 2
+    d_in.wait()
+    mask_in.wait()
+    mturn[...] = jnp.broadcast_to(mask_ref[...].astype(F32), (128, N)).T
+    for q in range(4):
+        mcol[q] = mturn[pl.ds(q, 256, stride=4), :]
+
+    def turn(k, carry):
+        g, p = k // 2, k % 2
         block = d[p, 0, pl.ds(g * PER, PER)].reshape(128, N).astype(F32)
-        lanes = pl.ds(pl.multiple_of(p * 128, 128), 128)
-        dt[g, :, lanes] = block.T.astype(BF16)
+        dturn[...] = block.T
+        for q in range(4):
+            dt[g, p, q] = dturn[pl.ds(q, 256, stride=4), :].astype(BF16)
         return carry
 
     lax.fori_loop(0, 4, turn, 0)
+    ytab_in.wait()
 
     up.wait()
     down.wait()
@@ -205,30 +224,48 @@
     def middle(g, carry):
         wait_all(land, x_recv, g)
 
-        def residual(kt, inner):
-            rows = pl.ds(pl.multiple_of(kt * 256, 256), 256)
-            c_part = dot(tab[0, rows, :], land[g])
-            s_part = dot(tab[1, rows, :], land[g])
-            keep = mcol[rows, :]
-            real = c_part[:, :128] + s_part[:, 128:] - dt[g, rows, :128].astype(F32)
-            imag = c_part[:, 128:] - s_part[:, :128] - dt[g, rows, 128:].astype(F32)
-            mis[rows, :128] = (keep * real).astype(BF16)
-            mis[rows, 128:] = (keep * imag).astype(BF16)
+        def spread(k, inner):
+            part = [land[g, pl.ds(pl.multiple_of(p * 256 + k * 32, 32), 32), :].astype(F32) for p in range(4)]
+            at = pl.multiple_of(k * 32, 32)
+            plus, minus = part[0] + part[2], part[0] - part[2]
+            other, cross = part[1] + part[3], part[1] - part[3]
+            turned = jnp.concatenate([cross[:, 128:], -cross[:, :128]], axis=1)
+            for q, value in enumerate((plus + other, minus + turned, plus - other, minus - turned)):
+                short = value.astype(BF16)
+                uq[q, pl.ds(at, 32), :] = short
+                uq[q, pl.ds(256 + at, 32), :128] = short[:, 128:]
+                uq[q, pl.ds(256 + at, 32), 128:] = -short[:, :128]
             return inner
 
-        lax.fori_loop(0, 4, residual, 0)
-
-        def back(step, inner):
-            jj = (my_y + step) % 4
-            rows = pl.ds(pl.multiple_of(jj * 256, 256), 256)
-            c_part = dot(tab[0, rows, :], mis[...])
-            s_part = dot(tab[1, rows, :], mis[...])
-            b[g, rows, :128] = (c_part[:, :128] - s_part[:, 128:]).astype(BF16)
-            b[g, rows, 128:] = (c_part[:, 128:] + s_part[:, :128]).astype(BF16)
-            send_eight(b, r, b_send, b_recv, g, jj)
+        lax.fori_loop(0, 8, spread, 0)
+        for q in range(4):
+            spectrum = dot(ytab[0, q], uq[q])
+            keep = mcol[q]
+            real = (keep * (spectrum[:, :128] - dt[g, 0, q].astype(F32))).astype(BF16)
+            imag = (keep * (spectrum[:, 128:] - dt[g, 1, q].astype(F32))).astype(BF16)
+            mis[q, :256, :128] = real
+            mis[q, :256, 128:] = imag
+            mis[q, 256:, :128] = -imag
+            mis[q, 256:, 128:] = real
+        for q in range(4):
+            bq[q] = dot(ytab[1, q], mis[q])
+
+        def back(k, inner):
+            at = pl.ds(pl.multiple_of(k * 32, 32), 32)
+            part = [bq[q, at, :] for q in range(4)]
+            plus, minus = part[0] + part[2], part[0] - part[2]
+            other, cross = part[1] + part[3], part[1] - part[3]
+            turned = jnp.concatenate([-cross[:, 128:], cross[:, :128]], axis=1)
+            for p, value in enumerate((plus + other, minus + turned, plus - other, minus - turned)):
+                to = pl.multiple_of(p * 256 + k * 32, 32)
+                b[g, pl.ds(to, 32), :] = value.astype(BF16)
+                send_rows(b, r, b_send, b_recv, g, p * 8 + k)
             return inner
 
-        lax.fori_loop(0, 4, back, 0)
+        def back_from(k, inner):
+            return back((row + k) % 8, inner)
+
+        lax.fori_loop(0, 8, back_from, 0)
         return carry
 
     lax.fori_loop(0, GROUPS, middle, 0)
@@ -243,18 +280,24 @@
                     r[g, pl.ds(pl.multiple_of((4 * j + i) * 32, 32), 32), p * 128:(p + 1) * 128].astype(F32)
                     for i in range(4)])
                 for c in range(4):
-                    lmat[p * 128 + c * 32:p * 128 + (c + 1) * 32, lanes] = got[c].astype(BF16)
+                    short = got[c].astype(BF16)
+                    other = pl.ds(pl.multiple_of(N + j * 128, 128), 128)
+                    line = slice(c * 32, (c + 1) * 32)
+                    cross = slice(128 + c * 32, 128 + (c + 1) * 32)
+                    if p == 0:
+                        lmat[line, lanes] = short
+                        lmat[cross, other] = short
+                    else:
+                        lmat[line, other] = -short
+                        lmat[cross, lanes] = short
             return carry
 
         lax.fori_loop(0, 8, gather, 0)
 
         def inverse_x(xt, carry):
             cols = pl.ds(pl.multiple_of(xt * 256, 256), 256)
-            lhs = lmat[...]
-            c_part = dot(lhs, tab[0, :, cols])
-            s_part = dot(lhs, tab[1, :, cols])
-            real = c_part[:128] - s_part[128:]
-            imag = c_part[128:] + s_part[:128]
+            both = dot(lmat[...], xtab[:, cols])
+            real, imag = both[:128], both[128:]
             gr = jnp.zeros((32, 256), F32)
             gi = jnp.zeros((32, 256), F32)
             for c in range(PER):
@@ -301,44 +344,75 @@
         wait_all(b, b_send, g)
 
 
-def outer_kernel(v_ref, g_ref, out_ref):
-    block = pl.program_id(1)
-    first = g_ref[0, 0]
-    second = g_ref[1, 0]
-    for k in range(out_ref.shape[1]):
-        at = block * out_ref.shape[1] + k
-        out_ref[0, k] = v_ref[0, at] * first + v_ref[1, at] * second
+def spread_column(values, which, column):
+    line = jnp.where(which == 0, values[0:1], values[1:2])
+    here = lax.broadcasted_iota(jnp.int32, (RANK, RANK), 0) == lax.broadcasted_iota(jnp.int32, (RANK, RANK), 1)
+    column[...] = dot(jnp.where(here, line, 0.0).astype(BF16), jnp.ones((RANK, column.shape[1]), BF16))
+
+
+def outer_kernel(v_hbm, g_hbm, out_hbm, v_ref, g_ref, first, second, out, in_sem, sem):
+    g_in = [pltpu.make_async_copy(g_hbm.at[:, p], g_ref.at[:, p], in_sem.at[p]) for p in range(2)]
+    v_in = pltpu.make_async_copy(v_hbm, v_ref, in_sem.at[2])
+    v_in.start()
+    for copy in g_in:
+        copy.start()
+    v_in.wait()
+    values = v_ref[...].astype(F32)
+    spread_column(values, 0, first)
+    spread_column(values, 1, second)
+    step = 4
+    for p in range(2):
+        g_in[p].wait()
+
+        def some(block, carry):
+            for top in range(0, ROWS, 8):
+                for half in range(0, N, 512):
+                    part = (slice(top, top + 8), slice(half, half + 512))
+                    g0 = g_ref[0, p, part[0], part[1]]
+                    g1 = g_ref[1, p, part[0], part[1]]
+                    for k in range(step):
+                        at = block * step + k
+                        out[p, at, part[0], part[1]] = first[pl.ds(at, 1), :] * g0 + second[pl.ds(at, 1), :] * g1
+            ranks = pl.ds(block * step, step)
+            pltpu.make_async_copy(out.at[p, ranks], out_hbm.at[p, ranks], sem).start()
+            return carry
+
+        lax.fori_loop(0, RANK // step, some, 0)
+    pltpu.make_async_copy(out, out_hbm, sem).wait()
 
 
 def shards(factor_u, temporal_v, sensitivity, kspace_data, sample_mask, tv_weight):
-    table = jnp.asarray(fourier_tables())
-    v = temporal_v.astype(F32)
-    anywhere = pl.BlockSpec(memory_space=pl.ANY)
+    anywhere = pl.BlockSpec(memory_space=pltpu.HBM)
     dma = pltpu.SemaphoreType.DMA
     combined = pl.pallas_call(
         main_kernel,
         out_shape=jax.ShapeDtypeStruct((2, 2, ROWS, N), F32),
-        in_specs=[
-            pl.BlockSpec(memory_space=pltpu.SMEM), pl.BlockSpec(memory_space=pltpu.VMEM),
-            anywhere, anywhere, anywhere, anywhere, anywhere,
-        ],
+        in_specs=[anywhere] * 8,
         out_specs=pl.BlockSpec(memory_space=pltpu.VMEM),
         scratch_shapes=[
             pltpu.VMEM((2, RANK, ROWS, N), BF16),
             pltpu.VMEM((2, COILS, ROWS, N), BF16),
             pltpu.VMEM((2, 1, COILS, ROWS, N), BF16),
             pltpu.VMEM((ROWS, N), F32),
-            pltpu.VMEM((2, N, N), BF16),
+            pltpu.VMEM((2 * N, N), BF16),
+            pltpu.VMEM((2, 4, 256, 512), BF16),
+            pltpu.VMEM((1, N), jnp.int32),
+            pltpu.VMEM((2, RANK), BF16),
+            pltpu.VMEM((RANK, 512), F32),
             pltpu.VMEM((2, ROWS, N), F32),
-            pltpu.VMEM((GROUPS, 256, N), BF16),
-            pltpu.VMEM((GROUPS, N, 256), BF16),
+            pltpu.VMEM((GROUPS, 256, 2 * N), BF16),
+            pltpu.VMEM((GROUPS, 2, 4, 256, 128), BF16),
+            pltpu.VMEM((N, 128), F32),
+            pltpu.VMEM((4, 256, 128), F32),
             pltpu.VMEM((N, 128), F32),
             pltpu.VMEM((GROUPS, N, 256), BF16),
             pltpu.VMEM((GROUPS, N, 256), BF16),
-            pltpu.VMEM((N, 256), BF16),
+            pltpu.VMEM((4, 512, 256), BF16),
+            pltpu.VMEM((4, 512, 256), BF16),
+            pltpu.VMEM((4, 256, 256), F32),
             pltpu.VMEM((GROUPS, N, 256), BF16),
             pltpu.VMEM((GROUPS, N, 256), BF16),
-            pltpu.VMEM((256, N), BF16),
+            pltpu.VMEM((256, 2 * N), BF16),
             pltpu.VMEM((2, ROWS, N), F32),
             pltpu.VMEM((2, 8, N), F32),
             pltpu.VMEM((2, 8, N), F32),
@@ -346,30 +420,30 @@
             pltpu.VMEM((4, 2, ROWS, 256), BF16),
             pltpu.VMEM((2, 4, 2, ROWS, 256), F32),
             pltpu.VMEM((2, ROWS, N), F32),
-            dma((4,)), dma((4,)), dma((2,)), dma((2,)),
+            dma((4,)), dma((7,)), dma((2,)), dma((2,)),
             dma((GROUPS,)), dma((GROUPS,)), dma((GROUPS,)), dma((GROUPS,)),
             dma((4,)), dma((4,)), dma((4,)), dma((4,)),
         ],
         compiler_params=pltpu.CompilerParams(
-            collective_id=0, has_side_effects=True, vmem_limit_bytes=48 * 1024 * 1024
+            collective_id=0, has_side_effects=True, vmem_limit_bytes=VMEM_LIMIT
         ),
-        cost_estimate=pl.CostEstimate(flops=9 * 10**9, bytes_accessed=14 * 10**6, transcendentals=40000),
+        cost_estimate=pl.CostEstimate(flops=6 * 10**9, bytes_accessed=14 * 10**6, transcendentals=40000),
         name="frame_gradient",
-    )(v, sample_mask, factor_u, sensitivity, kspace_data, tv_weight, table)
-    step = 12
+    )(temporal_v, sample_mask, factor_u, sensitivity, kspace_data, tv_weight, jnp.asarray(x_table()), jnp.asarray(y_tables()))
     return pl.pallas_call(
         outer_kernel,
         out_shape=jax.ShapeDtypeStruct((2, RANK, ROWS, N), F32),
-        grid=(2, RANK // step),
-        in_specs=[
-            pl.BlockSpec(memory_space=pltpu.SMEM),
-            pl.BlockSpec((2, 1, ROWS, N), lambda p, k: (0, p, 0, 0)),
+        in_specs=[anywhere] * 2,
+        out_specs=anywhere,
+        scratch_shapes=[
+            pltpu.VMEM((2, RANK), BF16), pltpu.VMEM((2, 2, ROWS, N), F32),
+            pltpu.VMEM((RANK, 512), F32), pltpu.VMEM((RANK, 512), F32),
+            pltpu.VMEM((2, RANK, ROWS, N), F32), dma((3,)), dma,
         ],
-        out_specs=pl.BlockSpec((1, step, ROWS, N), lambda p, k: (p, k, 0, 0)),
-        compiler_params=pltpu.CompilerParams(vmem_limit_bytes=24 * 1024 * 1024),
+        compiler_params=pltpu.CompilerParams(vmem_limit_bytes=VMEM_LIMIT),
         cost_estimate=pl.CostEstimate(flops=10**7, bytes_accessed=13 * 10**6, transcendentals=0),
         name="spread_over_rank",
-    )(v, combined)
+    )(temporal_v, combined)
 
 
 def solution(mesh):

time: 59.2 us -> 54.2 us (0.916)
  local copies, waits for them, and re-layouts: 4.04 us -> 0 us
  other arithmetic: 0.66 us -> 0 us
    unnamed x8 -> x0, local copies, waits for them, and re-layouts: 4.04 us -> none
    pallas_call x1, Pallas kernels: 6.46 us -> 5.59 us  [shards(): pl.pallas_call(outer_kernel, out_shape=jax.ShapeDtypeStruct((2, RANK, ROW...]
    pallas_call x1, Pallas kernels: 47.8 us -> 48.4 us  [shards(): pl.pallas_call(main_kernel, out_shape=jax.ShapeDtypeStruct((2, 2, ROWS, N...]
    convert_element_type x1 -> x0, other arithmetic: 0.66 us -> none  [shards(): v = temporal_v.astype(F32)]
where the time goes in v1:
time: 54.2 us; the launch traced here: 54 us
  Pallas kernels  54 us (100%)
    pallas_call x1, Pallas kernels, shards(): pl.pallas_call(main_kernel, out_shape=jax.ShapeDtypeStruct((2, 2, ROWS, N...  48.4 us
    pallas_call x1, Pallas kernels, shards(): pl.pallas_call(outer_kernel, out_shape=jax.ShapeDtypeStruct((2, RANK, ROW...  5.59 us

profile of v1, /device:TPU:1, one launch (start us, length us, event | category | flops | bytes accessed | tf_op | source)
XLA Modules:
  0.0 54.0 jit_solution(16267128308896338229)
XLA Ops:
  0.0 48.4 %frame_gradient.1.g_hbm = f32[2,2,32,1024]{3,2,1,0:T(8,128)} custom-call(bf16[2,48]{1,0:T(2,128)(2,1)} %v_hbm.3, s32[1,1024]{1,0:T(1,128)} %mask_hbm.1, bf16[2,48,32,1024]{3,2,1,0:T(8,128)(2,1)} %u_hbm.1, bf16[2,8,32,1024]{3,2,1,0:T(8,128)(2,1)} %s_hbm.1, bf16[2,1,8,32,1024]{4,3,2,1,0:T(8,128)(2,1)} %d_hbm.1, f32[32,1024]{1,0:T(8,128)} %w_hbm.1, ...), custom_call_target="tpu_custom_call" | custom-call | flops 6000000000 | bytes 14000000 | tf_op jit(solution)/shard_map/frame_gradient/pallas_call | solution.py:387
  48.4 5.6 %spread_over_rank.1 = f32[2,48,32,1024]{3,2,1,0:T(8,128)} custom-call(bf16[2,48]{1,0:T(2,128)(2,1)} %v_hbm.3, f32[2,2,32,1024]{3,2,1,0:T(8,128)} %frame_gradient.1.g_hbm), custom_call_target="tpu_custom_call" | custom-call | flops 10000000 | bytes 13000000 | tf_op jit(solution)/shard_map/spread_over_rank/pallas_call | solution.py:433

commit v2 on v1

--- a/solution.py
+++ b/solution.py
@@ -63,25 +63,23 @@
 
 def main_kernel(
     v_hbm, mask_hbm, u_hbm, s_hbm, d_hbm, w_hbm, xtab_hbm, ytab_hbm, out_ref,
-    u, s, d, w, xtab, ytab, mask_ref, v_ref, vcol, f, a, dt, dturn, mcol, mturn, x, land, uq, mis, bq, b, r, lmat, acc, halo_s, halo_r, part_s, part_r, comb, tvg,
-    u_sem, in_sem, halo_send, halo_recv, x_send, x_recv, b_send, b_recv, p_send, p_recv, c_send, c_recv,
+    u, s, d, w, xtab, ytab, mask_ref, v_ref, vcol, f, fs, fl, fy, dturn, mcol, x, land, uq, mis, bq, b, r,
+    gacc, gs, gl, lmat, acc, halo_s, halo_r, part_s, part_r, comb, tvg,
+    u_sem, in_sem, halo_send, halo_recv, s_send, s_recv, e_send, e_recv, f_send, f_recv, b_send, b_recv,
+    g_send, g_recv, p_send, p_recv, c_send, c_recv,
 ):
     row = lax.axis_index("row")
     frame = lax.axis_index("frame")
     coil = lax.axis_index("coil")
-    my_y = row // 8
-
-    in_copies = []
-    names = ((v_hbm, v_ref), (s_hbm, s), (w_hbm, w), (xtab_hbm, xtab), (mask_hbm, mask_ref), (d_hbm, d), (ytab_hbm, ytab))
-    for q, (src, dst) in enumerate(names):
-        in_copies.append(pltpu.make_async_copy(src, dst, in_sem.at[q]))
-    v_in, s_in, w_in, xtab_in, mask_in, d_in, ytab_in = in_copies
+
+    names = ((v_hbm, v_ref), (s_hbm, s), (mask_hbm, mask_ref), (d_hbm, d), (ytab_hbm, ytab), (w_hbm, w), (xtab_hbm, xtab))
+    in_copies = [pltpu.make_async_copy(src, dst, in_sem.at[q]) for q, (src, dst) in enumerate(names)]
+    v_in, s_in, mask_in, d_in, ytab_in, w_in, xtab_in = in_copies
     u_copies = []
     for q in range(4):
         part = (q // 2, slice(None), pl.ds((q % 2) * 16, 16))
         u_copies.append(pltpu.make_async_copy(u_hbm.at[part], u.at[part], u_sem.at[q]))
-    v_in.start()
-    for copy in u_copies + in_copies[1:]:
+    for copy in in_copies[:2] + u_copies + in_copies[2:]:
         copy.start()
 
     barrier = pltpu.get_barrier_semaphore()
@@ -95,6 +93,45 @@
     lax.fori_loop(0, DEVS, greet, 0)
     pl.semaphore_signal(barrier, inc=1, device_id={"coil": 1 - coil}, device_id_type=pl.DeviceIdType.MESH)
     pl.semaphore_signal(barrier, inc=1, device_id={"frame": 1 - frame}, device_id_type=pl.DeviceIdType.MESH)
+
+    def send_rows(src, dst, send_sem, recv_sem, size, to):
+        rows = pl.ds(pl.multiple_of(to * size, size), size)
+        mine = pl.ds(pl.multiple_of(row * size, size), size)
+
+        @pl.when(to != row)
+        def _():
+            pltpu.make_async_remote_copy(
+                src.at[rows], dst.at[mine], send_sem, recv_sem,
+                device_id={"row": to}, device_id_type=pl.DeviceIdType.MESH).start()
+
+        @pl.when(to == row)
+        def _():
+            dst[mine, :] = src[rows, :]
+
+    def wait_bytes(ref, sem):
+        pltpu.make_async_copy(ref, ref, sem).wait()
+
+    def wait_all(ref, sem):
+        wait_bytes(ref.at[pl.ds(0, ref.shape[0] // DEVS * (DEVS - 1))], sem)
+
+    s_in.wait()
+
+    def lay_maps(k, carry):
+        j = (row // 4 + k) % 8
+        lanes = pl.ds(pl.multiple_of(j * 128, 128), 128)
+        for p in range(2):
+            w4 = swap_blocks([s[p, frame * PER + c, :, lanes].astype(F32) for c in range(4)])
+            for i in range(4):
+                x[pl.ds(pl.multiple_of((j * 4 + i) * 32, 32), 32), p * 128:(p + 1) * 128] = w4[i].astype(BF16)
+        return carry
+
+    def send_maps(k, carry):
+        send_rows(x, land.at[frame], s_send.at[0], s_recv.at[0], 32, (row + k) % DEVS)
+        return carry
+
+    lax.fori_loop(0, 8, lay_maps, 0)
+    pl.semaphore_wait(barrier, DEVS + 1)
+    lax.fori_loop(0, DEVS, send_maps, 0)
 
     v_in.wait()
     spread_column(v_ref[...].astype(F32), frame, vcol)
@@ -107,32 +144,24 @@
                 total += vcol[k:k + 1, :] * u[p, k, top:top + 16, half * 512:(half + 1) * 512].astype(F32)
             f[p, top:top + 16, half * 512:(half + 1) * 512] = total
 
-    s_in.wait()
+    def send_frame(k, carry):
+        j = (row // 4 + k) % 8
+        lanes = pl.ds(pl.multiple_of(j * 128, 128), 128)
+        w4 = swap_blocks([f[hp % 2, hp // 2 * 16:hp // 2 * 16 + 16, lanes] for hp in range(4)])
+        for i in range(4):
+            to = j * 4 + i
+            fs[pl.ds(pl.multiple_of(to * 16, 16), 16), :] = w4[i].astype(BF16)
+            send_rows(fs, fl, f_send.at[0], f_recv.at[0], 16, to)
+        return carry
+
+    lax.fori_loop(0, 8, send_frame, 0)
+
     w_in.wait()
     halo_s[...] = jnp.zeros_like(halo_s)
     for p in range(2):
         halo_s[0, p:p + 1, :] = f[p, 0:1, :]
         halo_s[1, p:p + 1, :] = f[p, 31:32, :]
     halo_s[1, 2:3, :] = w[31:32, :]
-
-    def coil_images(c, carry):
-        sr = s[0, c].astype(F32)
-        si = s[1, c].astype(F32)
-        fr, fi = f[0], f[1]
-        at = pl.multiple_of((c % PER) * 32, 32)
-        real = (sr * fr - si * fi).astype(BF16)
-        imag = (sr * fi + si * fr).astype(BF16)
-        a[c // PER, pl.ds(at, 32), :N] = real
-        a[c // PER, pl.ds(at, 32), N:] = imag
-        a[c // PER, pl.ds(128 + at, 32), :N] = imag
-        a[c // PER, pl.ds(128 + at, 32), N:] = -real
-        return carry
-
-    lax.fori_loop(0, COILS, coil_images, 0)
-    xtab_in.wait()
-
-    pl.semaphore_wait(barrier, DEVS + 1)
-
     up = pltpu.make_async_remote_copy(
         halo_s.at[0], halo_r.at[1], halo_send.at[0], halo_recv.at[1],
         device_id={"row": (row + DEVS - 1) % DEVS}, device_id_type=pl.DeviceIdType.MESH)
@@ -142,58 +171,47 @@
     up.start()
     down.start()
 
-    def send_rows(src, dst, send_sem, recv_sem, g, to):
-        rows = pl.ds(pl.multiple_of(to * 32, 32), 32)
-        mine = pl.ds(pl.multiple_of(row * 32, 32), 32)
-
-        @pl.when(to != row)
-        def _():
-            pltpu.make_async_remote_copy(
-                src.at[g, rows], dst.at[g, mine], send_sem.at[g], recv_sem.at[g],
-                device_id={"row": to}, device_id_type=pl.DeviceIdType.MESH).start()
-
-        @pl.when(to == row)
-        def _():
-            dst[g, mine, :] = src[g, mine, :]
-
-    def wait_all(ref, sem, g):
-        view = ref.at[g, pl.ds(0, N - 32)]
-        pltpu.make_async_copy(view, view, sem.at[g]).wait()
-
-    def forward_x(q, carry):
-        g, step = q // 4, q % 4
-        jj = (my_y + step) % 4
-        cols = pl.ds(pl.multiple_of(jj * 256, 256), 256)
-        both = dot(a[g], xtab[:, cols])
-        for p in range(2):
-            for h in range(2):
-                w4 = swap_blocks([both[p * 128 + c * 32:p * 128 + (c + 1) * 32, h * 128:(h + 1) * 128] for c in range(4)])
-                for i in range(4):
-                    at = pl.multiple_of((jj * 8 + h * 4 + i) * 32, 32)
-                    x[g, pl.ds(at, 32), p * 128:(p + 1) * 128] = w4[i].astype(BF16)
-        for k in range(8):
-            send_rows(x, land, x_send, x_recv, g, jj * 8 + k)
-        return carry
-
-    lax.fori_loop(0, 8, forward_x, 0)
-
     d_in.wait()
     mask_in.wait()
-    mturn[...] = jnp.broadcast_to(mask_ref[...].astype(F32), (128, N)).T
+    ytab_in.wait()
+
+    def fold_back(at):
+        part = [bq[q, at, :] for q in range(4)]
+        plus, minus = part[0] + part[2], part[0] - part[2]
+        other, cross = part[1] + part[3], part[1] - part[3]
+        turned = jnp.concatenate([-cross[:, 128:], cross[:, :128]], axis=1)
+        return plus + other, minus + turned, plus - other, minus - turned
+
+    def measured(g, carry):
+        keep = -mask_ref[...].astype(F32)
+        for p in range(2):
+            dturn[...] = (d[p, 0, pl.ds(g * PER, PER)].reshape(128, N).astype(F32) * keep).T
+            for q in range(4):
+                value = dturn[pl.ds(q, 256, stride=4), :].astype(BF16)
+                if p == 0:
+                    mis[q, :256, :128] = value
+                    mis[q, 256:, 128:] = value
+                else:
+                    mis[q, :256, 128:] = value
+                    mis[q, 256:, :128] = -value
+        for q in range(4):
+            bq[q] = dot(ytab[1, q], mis[q])
+
+        def back(k, inner):
+            turn = (row + k) % 8
+            for p, value in enumerate(fold_back(pl.ds(pl.multiple_of(turn * 32, 32), 32))):
+                b[g, pl.ds(pl.multiple_of(p * 256 + turn * 32, 32), 32), :] = value.astype(BF16)
+                send_rows(b.at[g], r.at[g], b_send.at[g], b_recv.at[g], 32, p * 8 + turn)
+            return inner
+
+        lax.fori_loop(0, 8, back, 0)
+        return carry
+
+    lax.fori_loop(0, GROUPS, measured, 0)
+
+    dturn[...] = jnp.broadcast_to(mask_ref[...].astype(F32), (128, N)).T
     for q in range(4):
-        mcol[q] = mturn[pl.ds(q, 256, stride=4), :]
-
-    def turn(k, carry):
-        g, p = k // 2, k % 2
-        block = d[p, 0, pl.ds(g * PER, PER)].reshape(128, N).astype(F32)
-        dturn[...] = block.T
-        for q in range(4):
-            dt[g, p, q] = dturn[pl.ds(q, 256, stride=4), :].astype(BF16)
-        return carry
-
-    lax.fori_loop(0, 4, turn, 0)
-    ytab_in.wait()
-
+        mcol[q] = dturn[pl.ds(q, 256, stride=4), :]
     up.wait()
     down.wait()
     lane = lax.broadcasted_iota(jnp.int32, (ROWS, N), 1)
@@ -221,28 +239,60 @@
         over = jnp.where(line == 0, top, pltpu.roll(fd, 1, 0))
         tvg[p] = TV_GAIN * ((left - fa) + (over - fd))
 
-    def middle(g, carry):
-        wait_all(land, x_recv, g)
+    wait_all(land.at[frame], s_recv.at[0])
+    share = pltpu.make_async_remote_copy(
+        land.at[frame], land.at[frame], e_send.at[0], e_recv.at[0],
+        device_id={"frame": 1 - frame}, device_id_type=pl.DeviceIdType.MESH)
+    share.start()
+    wait_all(fl, f_recv.at[0])
+    source = lax.broadcasted_iota(jnp.int32, (128, 512), 0)
+    target = lax.broadcasted_iota(jnp.int32, (128, 512), 1)
+    same = (source // 32 == target // 128) & (source % 32 == target % 32)
+    copies = jnp.where(same, 1.0, 0.0).astype(BF16)
+    fy[...] = dot(fl[...], copies)
+
+    def pencil(turn_g, carry):
+        g = (frame + turn_g) % 2
+
+        @pl.when(turn_g == 1)
+        def _():
+            wait_bytes(land.at[1 - frame], e_recv.at[0])
 
         def spread(k, inner):
-            part = [land[g, pl.ds(pl.multiple_of(p * 256 + k * 32, 32), 32), :].astype(F32) for p in range(4)]
+            part = []
+            for p in range(4):
+                at = p * 8 + k
+                maps = land[g, pl.ds(pl.multiple_of(at * 32, 32), 32), :].astype(F32)
+                image = fy[pl.ds(pl.multiple_of(at * 16, 16), 16), :]
+                fr = jnp.concatenate([image[:, :128], image[:, 256:384]], axis=0)
+                fi = jnp.concatenate([image[:, 128:256], image[:, 384:]], axis=0)
+                sr, si = maps[:, :128], maps[:, 128:]
+                part.append((sr * fr - si * fi, sr * fi + si * fr))
+            plus = [part[0][z] + part[2][z] for z in range(2)]
+            minus = [part[0][z] - part[2][z] for z in range(2)]
+            other = [part[1][z] + part[3][z] for z in range(2)]
+            cross = [part[1][z] - part[3][z] for z in range(2)]
+            values = (
+                (plus[0] + other[0], plus[1] + other[1]),
+                (minus[0] + cross[1], minus[1] - cross[0]),
+                (plus[0] - other[0], plus[1] - other[1]),
+                (minus[0] - cross[1], minus[1] + cross[0]),
+            )
             at = pl.multiple_of(k * 32, 32)
-            plus, minus = part[0] + part[2], part[0] - part[2]
-            other, cross = part[1] + part[3], part[1] - part[3]
-            turned = jnp.concatenate([cross[:, 128:], -cross[:, :128]], axis=1)
-            for q, value in enumerate((plus + other, minus + turned, plus - other, minus - turned)):
-                short = value.astype(BF16)
-                uq[q, pl.ds(at, 32), :] = short
-                uq[q, pl.ds(256 + at, 32), :128] = short[:, 128:]
-                uq[q, pl.ds(256 + at, 32), 128:] = -short[:, :128]
+            for q, (real, imag) in enumerate(values):
+                real, imag = real.astype(BF16), imag.astype(BF16)
+                uq[q, pl.ds(at, 32), :128] = real
+                uq[q, pl.ds(at, 32), 128:] = imag
+                uq[q, pl.ds(256 + at, 32), :128] = imag
+                uq[q, pl.ds(256 + at, 32), 128:] = -real
             return inner
 
         lax.fori_loop(0, 8, spread, 0)
         for q in range(4):
             spectrum = dot(ytab[0, q], uq[q])
             keep = mcol[q]
-            real = (keep * (spectrum[:, :128] - dt[g, 0, q].astype(F32))).astype(BF16)
-            imag = (keep * (spectrum[:, 128:] - dt[g, 1, q].astype(F32))).astype(BF16)
+            real = (keep * spectrum[:, :128]).astype(BF16)
+            imag = (keep * spectrum[:, 128:]).astype(BF16)
             mis[q, :256, :128] = real
             mis[q, :256, 128:] = imag
             mis[q, 256:, :128] = -imag
@@ -250,28 +300,43 @@
         for q in range(4):
             bq[q] = dot(ytab[1, q], mis[q])
 
-        def back(k, inner):
-            at = pl.ds(pl.multiple_of(k * 32, 32), 32)
-            part = [bq[q, at, :] for q in range(4)]
-            plus, minus = part[0] + part[2], part[0] - part[2]
-            other, cross = part[1] + part[3], part[1] - part[3]
-            turned = jnp.concatenate([-cross[:, 128:], cross[:, :128]], axis=1)
-            for p, value in enumerate((plus + other, minus + turned, plus - other, minus - turned)):
-                to = pl.multiple_of(p * 256 + k * 32, 32)
-                b[g, pl.ds(to, 32), :] = value.astype(BF16)
-                send_rows(b, r, b_send, b_recv, g, p * 8 + k)
+        def collect(k, inner):
+            turn = (row + k) % 8
+            for p, value in enumerate(fold_back(pl.ds(pl.multiple_of(turn * 32, 32), 32))):
+                to = p * 8 + turn
+                rows = pl.ds(pl.multiple_of(to * 32, 32), 32)
+                maps = land[g, rows, :].astype(F32)
+                sr, si = maps[:, :128], maps[:, 128:]
+                ar, ai = value[:, :128], value[:, 128:]
+                gr = sr * ar + si * ai
+                gi = sr * ai - si * ar
+
+                @pl.when(turn_g == 0)
+                def _():
+                    gacc[rows, :128] = gr
+                    gacc[rows, 128:] = gi
+
+                @pl.when(turn_g == 1)
+                def _():
+                    whole = []
+                    for z in (gacc[rows, :128] + gr, gacc[rows, 128:] + gi):
+                        z = z + pltpu.roll(z, 64, 1)
+                        whole.append(z + pltpu.roll(z, 32, 1))
+                    block = lax.broadcasted_iota(jnp.int32, (16, 128), 1) // 32
+                    upper = jnp.where(block == 0, whole[0][:16], whole[1][:16])
+                    lower = jnp.where(block == 2, whole[0][16:], whole[1][16:])
+                    gs[pl.ds(pl.multiple_of(to * 16, 16), 16), :] = jnp.where(block < 2, upper, lower).astype(BF16)
+                    send_rows(gs, gl, g_send.at[0], g_recv.at[0], 16, to)
             return inner
 
-        def back_from(k, inner):
-            return back((row + k) % 8, inner)
-
-        lax.fori_loop(0, 8, back_from, 0)
-        return carry
-
-    lax.fori_loop(0, GROUPS, middle, 0)
-
+        lax.fori_loop(0, 8, collect, 0)
+        return carry
+
+    lax.fori_loop(0, 2, pencil, 0)
+
+    xtab_in.wait()
     for g in range(GROUPS):
-        wait_all(r, b_recv, g)
+        wait_all(r.at[g], b_recv.at[g])
 
         def gather(j, carry):
             lanes = pl.ds(pl.multiple_of(j * 128, 128), 128)
@@ -293,6 +358,19 @@
             return carry
 
         lax.fori_loop(0, 8, gather, 0)
+
+        if g == GROUPS - 1:
+            wait_all(gl, g_recv.at[0])
+
+            def unpack(j, carry):
+                lanes = pl.ds(pl.multiple_of(j * 128, 128), 128)
+                got = swap_blocks([
+                    gl[pl.ds(pl.multiple_of((4 * j + i) * 16, 16), 16), :].astype(F32) for i in range(4)])
+                for hp in range(4):
+                    acc[hp % 2, hp // 2 * 16:hp // 2 * 16 + 16, lanes] += got[hp]
+                return carry
+
+            lax.fori_loop(0, 8, unpack, 0)
 
         def inverse_x(xt, carry):
             cols = pl.ds(pl.multiple_of(xt * 256, 256), 256)
@@ -321,11 +399,10 @@
         lax.fori_loop(0, 4, inverse_x, 0)
 
     def finish(xt, carry):
-        pltpu.make_async_copy(part_r.at[xt], part_r.at[xt], p_recv.at[xt]).wait()
+        wait_bytes(part_r.at[xt], p_recv.at[xt])
         cols = pl.ds(pl.multiple_of(xt * 256, 256), 256)
         for p in range(2):
-            whole = part_s[xt, p].astype(F32) + part_r[xt, p].astype(F32) + tvg[p, :, cols]
-            comb[frame, xt, p] = whole
+            comb[frame, xt, p] = part_s[xt, p].astype(F32) + part_r[xt, p].astype(F32) + tvg[p, :, cols]
         pltpu.make_async_remote_copy(
             comb.at[frame, xt], comb.at[frame, xt], c_send.at[xt], c_recv.at[xt],
             device_id={"frame": 1 - frame}, device_id_type=pl.DeviceIdType.MESH).start()
@@ -333,15 +410,19 @@
 
     lax.fori_loop(0, 4, finish, 0)
     for xt in range(4):
-        pltpu.make_async_copy(comb.at[1 - frame, xt], comb.at[1 - frame, xt], c_recv.at[xt]).wait()
-        pltpu.make_async_copy(comb.at[frame, xt], comb.at[frame, xt], c_send.at[xt]).wait()
-        pltpu.make_async_copy(part_s.at[xt], part_s.at[xt], p_send.at[xt]).wait()
+        wait_bytes(comb.at[1 - frame, xt], c_recv.at[xt])
         for t in range(2):
             for p in range(2):
                 out_ref[t, p, :, xt * 256:(xt + 1) * 256] = comb[t, xt, p]
+    for xt in range(4):
+        wait_bytes(comb.at[frame, xt], c_send.at[xt])
+        wait_bytes(part_s.at[xt], p_send.at[xt])
+    wait_all(x, s_send.at[0])
+    wait_all(fs, f_send.at[0])
+    wait_all(gs, g_send.at[0])
+    share.wait_send()
     for g in range(GROUPS):
-        wait_all(x, x_send, g)
-        wait_all(b, b_send, g)
+        wait_all(b.at[g], b_send.at[g])
 
 
 def spread_column(values, which, column):
@@ -400,18 +481,21 @@
             pltpu.VMEM((2, RANK), BF16),
             pltpu.VMEM((RANK, 512), F32),
             pltpu.VMEM((2, ROWS, N), F32),
-            pltpu.VMEM((GROUPS, 256, 2 * N), BF16),
-            pltpu.VMEM((GROUPS, 2, 4, 256, 128), BF16),
+            pltpu.VMEM((N // 2, 128), BF16),
+            pltpu.VMEM((N // 2, 128), BF16),
+            pltpu.VMEM((N // 2, 512), F32),
             pltpu.VMEM((N, 128), F32),
             pltpu.VMEM((4, 256, 128), F32),
-            pltpu.VMEM((N, 128), F32),
-            pltpu.VMEM((GROUPS, N, 256), BF16),
+            pltpu.VMEM((N, 256), BF16),
             pltpu.VMEM((GROUPS, N, 256), BF16),
             pltpu.VMEM((4, 512, 256), BF16),
             pltpu.VMEM((4, 512, 256), BF16),
             pltpu.VMEM((4, 256, 256), F32),
             pltpu.VMEM((GROUPS, N, 256), BF16),
             pltpu.VMEM((GROUPS, N, 256), BF16),
+            pltpu.VMEM((N, 256), F32),
+            pltpu.VMEM((N // 2, 128), BF16),
+            pltpu.VMEM((N // 2, 128), BF16),
             pltpu.VMEM((256, 2 * N), BF16),
             pltpu.VMEM((2, ROWS, N), F32),
             pltpu.VMEM((2, 8, N), F32),
@@ -421,8 +505,8 @@
             pltpu.VMEM((2, 4, 2, ROWS, 256), F32),
             pltpu.VMEM((2, ROWS, N), F32),
             dma((4,)), dma((7,)), dma((2,)), dma((2,)),
-            dma((GROUPS,)), dma((GROUPS,)), dma((GROUPS,)), dma((GROUPS,)),
-            dma((4,)), dma((4,)), dma((4,)), dma((4,)),
+            dma((1,)), dma((1,)), dma((1,)), dma((1,)), dma((1,)), dma((1,)), dma((GROUPS,)), dma((GROUPS,)),
+            dma((1,)), dma((1,)), dma((4,)), dma((4,)), dma((4,)), dma((4,)),
         ],
         compiler_params=pltpu.CompilerParams(
             collective_id=0, has_side_effects=True, vmem_limit_bytes=VMEM_LIMIT

time: 54.2 us -> 52.7 us (0.972)
  Pallas kernels: 54 us -> 52.6 us
    pallas_call x1, Pallas kernels: 48.4 us -> 47 us  [shards(): pl.pallas_call(main_kernel, out_shape=jax.ShapeDtypeStruct((2, 2, ROWS, N...]
where the time goes in v2:
time: 52.7 us; the launch traced here: 52.6 us
  Pallas kernels  52.6 us (100%)
    pallas_call x1, Pallas kernels, shards(): pl.pallas_call(main_kernel, out_shape=jax.ShapeDtypeStruct((2, 2, ROWS, N...  47 us
    pallas_call x1, Pallas kernels, shards(): pl.pallas_call(outer_kernel, out_shape=jax.ShapeDtypeStruct((2, RANK, ROW...  5.59 us

profile of v2, /device:TPU:1, one launch (start us, length us, event | category | flops | bytes accessed | tf_op | source)
XLA Modules:
  0.0 52.6 jit_solution(16817624227736725039)
XLA Ops:
  0.0 47.0 %frame_gradient.1.g_hbm = f32[2,2,32,1024]{3,2,1,0:T(8,128)} custom-call(bf16[2,48]{1,0:T(2,128)(2,1)} %v_hbm.3, s32[1,1024]{1,0:T(1,128)} %mask_hbm.1, bf16[2,48,32,1024]{3,2,1,0:T(8,128)(2,1)} %u_hbm.1, bf16[2,8,32,1024]{3,2,1,0:T(8,128)(2,1)} %s_hbm.1, bf16[2,1,8,32,1024]{4,3,2,1,0:T(8,128)(2,1)} %d_hbm.1, f32[32,1024]{1,0:T(8,128)} %w_hbm.1, ...), custom_call_target="tpu_custom_call" | custom-call | flops 6000000000 | bytes 14000000 | tf_op jit(solution)/shard_map/frame_gradient/pallas_call | solution.py:468
  47.0 5.6 %spread_over_rank.1 = f32[2,48,32,1024]{3,2,1,0:T(8,128)} custom-call(bf16[2,48]{1,0:T(2,128)(2,1)} %v_hbm.3, f32[2,2,32,1024]{3,2,1,0:T(8,128)} %frame_gradient.1.g_hbm), custom_call_target="tpu_custom_call" | custom-call | flops 10000000 | bytes 13000000 | tf_op jit(solution)/shard_map/spread_over_rank/pallas_call | solution.py:517

commit v3 on v2

--- a/solution.py
+++ b/solution.py
@@ -62,11 +62,11 @@
 
 
 def main_kernel(
-    v_hbm, mask_hbm, u_hbm, s_hbm, d_hbm, w_hbm, xtab_hbm, ytab_hbm, out_ref,
+    v_hbm, mask_hbm, u_hbm, s_hbm, d_hbm, w_hbm, xtab_hbm, ytab_hbm, out_hbm,
     u, s, d, w, xtab, ytab, mask_ref, v_ref, vcol, f, fs, fl, fy, dturn, mcol, x, land, uq, mis, bq, b, r,
     gacc, gs, gl, lmat, acc, halo_s, halo_r, part_s, part_r, comb, tvg,
     u_sem, in_sem, halo_send, halo_recv, s_send, s_recv, e_send, e_recv, f_send, f_recv, b_send, b_recv,
-    g_send, g_recv, p_send, p_recv, c_send, c_recv,
+    g_send, g_recv, p_send, p_recv, c_send, c_recv, o_sem,
 ):
     row = lax.axis_index("row")
     frame = lax.axis_index("frame")
@@ -94,19 +94,18 @@
     pl.semaphore_signal(barrier, inc=1, device_id={"coil": 1 - coil}, device_id_type=pl.DeviceIdType.MESH)
     pl.semaphore_signal(barrier, inc=1, device_id={"frame": 1 - frame}, device_id_type=pl.DeviceIdType.MESH)
 
-    def send_rows(src, dst, send_sem, recv_sem, size, to):
-        rows = pl.ds(pl.multiple_of(to * size, size), size)
+    def send_all(src, dst, send_sem, recv_sem, size):
         mine = pl.ds(pl.multiple_of(row * size, size), size)
 
-        @pl.when(to != row)
-        def _():
+        def send(k, carry):
+            to = (row + 13 * k) % DEVS
             pltpu.make_async_remote_copy(
-                src.at[rows], dst.at[mine], send_sem, recv_sem,
+                src.at[pl.ds(pl.multiple_of(to * size, size), size)], dst.at[mine], send_sem, recv_sem,
                 device_id={"row": to}, device_id_type=pl.DeviceIdType.MESH).start()
-
-        @pl.when(to == row)
-        def _():
-            dst[mine, :] = src[rows, :]
+            return carry
+
+        lax.fori_loop(1, DEVS, send, 0)
+        dst[mine, :] = src[mine, :]
 
     def wait_bytes(ref, sem):
         pltpu.make_async_copy(ref, ref, sem).wait()
@@ -117,21 +116,17 @@
     s_in.wait()
 
     def lay_maps(k, carry):
-        j = (row // 4 + k) % 8
+        j = k
         lanes = pl.ds(pl.multiple_of(j * 128, 128), 128)
         for p in range(2):
-            w4 = swap_blocks([s[p, frame * PER + c, :, lanes].astype(F32) for c in range(4)])
+            w4 = swap_blocks([s[p, frame * PER + c, :, lanes] for c in range(4)])
             for i in range(4):
-                x[pl.ds(pl.multiple_of((j * 4 + i) * 32, 32), 32), p * 128:(p + 1) * 128] = w4[i].astype(BF16)
-        return carry
-
-    def send_maps(k, carry):
-        send_rows(x, land.at[frame], s_send.at[0], s_recv.at[0], 32, (row + k) % DEVS)
+                x[pl.ds(pl.multiple_of((j * 4 + i) * 32, 32), 32), p * 128:(p + 1) * 128] = w4[i]
         return carry
 
     lax.fori_loop(0, 8, lay_maps, 0)
     pl.semaphore_wait(barrier, DEVS + 1)
-    lax.fori_loop(0, DEVS, send_maps, 0)
+    send_all(x, land.at[frame], s_send.at[0], s_recv.at[0], 32)
 
     v_in.wait()
     spread_column(v_ref[...].astype(F32), frame, vcol)
@@ -145,16 +140,16 @@
             f[p, top:top + 16, half * 512:(half + 1) * 512] = total
 
     def send_frame(k, carry):
-        j = (row // 4 + k) % 8
+        j = k
         lanes = pl.ds(pl.multiple_of(j * 128, 128), 128)
         w4 = swap_blocks([f[hp % 2, hp // 2 * 16:hp // 2 * 16 + 16, lanes] for hp in range(4)])
         for i in range(4):
             to = j * 4 + i
             fs[pl.ds(pl.multiple_of(to * 16, 16), 16), :] = w4[i].astype(BF16)
-            send_rows(fs, fl, f_send.at[0], f_recv.at[0], 16, to)
         return carry
 
     lax.fori_loop(0, 8, send_frame, 0)
+    send_all(fs, fl, f_send.at[0], f_recv.at[0], 16)
 
     w_in.wait()
     halo_s[...] = jnp.zeros_like(halo_s)
@@ -198,64 +193,50 @@
             bq[q] = dot(ytab[1, q], mis[q])
 
         def back(k, inner):
-            turn = (row + k) % 8
+            turn = k
             for p, value in enumerate(fold_back(pl.ds(pl.multiple_of(turn * 32, 32), 32))):
                 b[g, pl.ds(pl.multiple_of(p * 256 + turn * 32, 32), 32), :] = value.astype(BF16)
-                send_rows(b.at[g], r.at[g], b_send.at[g], b_recv.at[g], 32, p * 8 + turn)
             return inner
 
         lax.fori_loop(0, 8, back, 0)
         return carry
 
+    def send_measured(g):
+        mine = pl.ds(pl.multiple_of(row * 32, 32), 32)
+        own = pltpu.make_async_copy(b.at[g, mine], r.at[g, mine], b_recv.at[g, row // 4])
+
+        def send(k, carry):
+            to = (row + 13 * k) % DEVS
+            pltpu.make_async_remote_copy(
+                b.at[g, pl.ds(pl.multiple_of(to * 32, 32), 32)], r.at[g, mine], b_send.at[g], b_recv.at[g, row // 4],
+                device_id={"row": to}, device_id_type=pl.DeviceIdType.MESH).start()
+            return carry
+
+        lax.fori_loop(1, DEVS, send, 0)
+        own.start()
+
     lax.fori_loop(0, GROUPS, measured, 0)
+    send_measured(0)
 
     dturn[...] = jnp.broadcast_to(mask_ref[...].astype(F32), (128, N)).T
     for q in range(4):
         mcol[q] = dturn[pl.ds(q, 256, stride=4), :]
-    up.wait()
-    down.wait()
-    lane = lax.broadcasted_iota(jnp.int32, (ROWS, N), 1)
-    line = lax.broadcasted_iota(jnp.int32, (ROWS, N), 0)
-    last_col = lane == N - 1
-    last_line = line == ROWS - 1
-    across, downs = [], []
-    for p in range(2):
-        cur = f[p]
-        across.append(jnp.where(last_col, 0.0, pltpu.roll(cur, N - 1, 1) - cur))
-        below = jnp.where(last_line, halo_r[1, p:p + 1, :], pltpu.roll(cur, ROWS - 1, 0))
-        downs.append(jnp.where(last_line & (row == DEVS - 1), 0.0, below - cur))
-    scale = w[...] / jnp.sqrt(across[0] * across[0] + across[1] * across[1]
-                              + downs[0] * downs[0] + downs[1] * downs[1] + TV_EPS)
-    above = halo_r[0]
-    top_across = jnp.where(lax.broadcasted_iota(jnp.int32, (8, N), 1) == N - 1, 0.0, pltpu.roll(above, N - 1, 1) - above)
-    top_down = [f[p, 0:1, :] - above[p:p + 1] for p in range(2)]
-    top_scale = above[2:3] / jnp.sqrt(top_across[0:1] * top_across[0:1] + top_across[1:2] * top_across[1:2]
-                                      + top_down[0] * top_down[0] + top_down[1] * top_down[1] + TV_EPS)
-    for p in range(2):
-        fa = scale * across[p]
-        fd = scale * downs[p]
-        top = jnp.where(row == 0, 0.0, top_scale * top_down[p])
-        left = jnp.where(lane == 0, 0.0, pltpu.roll(fa, 1, 1))
-        over = jnp.where(line == 0, top, pltpu.roll(fd, 1, 0))
-        tvg[p] = TV_GAIN * ((left - fa) + (over - fd))
-
     wait_all(land.at[frame], s_recv.at[0])
     share = pltpu.make_async_remote_copy(
         land.at[frame], land.at[frame], e_send.at[0], e_recv.at[0],
         device_id={"frame": 1 - frame}, device_id_type=pl.DeviceIdType.MESH)
     share.start()
     wait_all(fl, f_recv.at[0])
+    send_measured(1)
     source = lax.broadcasted_iota(jnp.int32, (128, 512), 0)
     target = lax.broadcasted_iota(jnp.int32, (128, 512), 1)
     same = (source // 32 == target // 128) & (source % 32 == target % 32)
     copies = jnp.where(same, 1.0, 0.0).astype(BF16)
     fy[...] = dot(fl[...], copies)
 
-    def pencil(turn_g, carry):
+    for turn_g in range(2):
         g = (frame + turn_g) % 2
-
-        @pl.when(turn_g == 1)
-        def _():
+        if turn_g == 1:
             wait_bytes(land.at[1 - frame], e_recv.at[0])
 
         def spread(k, inner):
@@ -301,7 +282,7 @@
             bq[q] = dot(ytab[1, q], mis[q])
 
         def collect(k, inner):
-            turn = (row + k) % 8
+            turn = k
             for p, value in enumerate(fold_back(pl.ds(pl.multiple_of(turn * 32, 32), 32))):
                 to = p * 8 + turn
                 rows = pl.ds(pl.multiple_of(to * 32, 32), 32)
@@ -311,13 +292,10 @@
                 gr = sr * ar + si * ai
                 gi = sr * ai - si * ar
 
-                @pl.when(turn_g == 0)
-                def _():
+                if turn_g == 0:
                     gacc[rows, :128] = gr
                     gacc[rows, 128:] = gi
-
-                @pl.when(turn_g == 1)
-                def _():
+                else:
                     whole = []
                     for z in (gacc[rows, :128] + gr, gacc[rows, 128:] + gi):
                         z = z + pltpu.roll(z, 64, 1)
@@ -326,26 +304,51 @@
                     upper = jnp.where(block == 0, whole[0][:16], whole[1][:16])
                     lower = jnp.where(block == 2, whole[0][16:], whole[1][16:])
                     gs[pl.ds(pl.multiple_of(to * 16, 16), 16), :] = jnp.where(block < 2, upper, lower).astype(BF16)
-                    send_rows(gs, gl, g_send.at[0], g_recv.at[0], 16, to)
             return inner
 
         lax.fori_loop(0, 8, collect, 0)
-        return carry
-
-    lax.fori_loop(0, 2, pencil, 0)
+    send_all(gs, gl, g_send.at[0], g_recv.at[0], 16)
+
+    up.wait()
+    down.wait()
+    lane = lax.broadcasted_iota(jnp.int32, (ROWS, N), 1)
+    line = lax.broadcasted_iota(jnp.int32, (ROWS, N), 0)
+    last_col = lane == N - 1
+    last_line = line == ROWS - 1
+    across, downs = [], []
+    for p in range(2):
+        cur = f[p]
+        across.append(jnp.where(last_col, 0.0, pltpu.roll(cur, N - 1, 1) - cur))
+        below = jnp.where(last_line, halo_r[1, p:p + 1, :], pltpu.roll(cur, ROWS - 1, 0))
+        downs.append(jnp.where(last_line & (row == DEVS - 1), 0.0, below - cur))
+    scale = w[...] / jnp.sqrt(across[0] * across[0] + across[1] * across[1]
+                              + downs[0] * downs[0] + downs[1] * downs[1] + TV_EPS)
+    above = halo_r[0]
+    top_across = jnp.where(lax.broadcasted_iota(jnp.int32, (8, N), 1) == N - 1, 0.0, pltpu.roll(above, N - 1, 1) - above)
+    top_down = [f[p, 0:1, :] - above[p:p + 1] for p in range(2)]
+    top_scale = above[2:3] / jnp.sqrt(top_across[0:1] * top_across[0:1] + top_across[1:2] * top_across[1:2]
+                                      + top_down[0] * top_down[0] + top_down[1] * top_down[1] + TV_EPS)
+    for p in range(2):
+        fa = scale * across[p]
+        fd = scale * downs[p]
+        top = jnp.where(row == 0, 0.0, top_scale * top_down[p])
+        left = jnp.where(lane == 0, 0.0, pltpu.roll(fa, 1, 1))
+        over = jnp.where(line == 0, top, pltpu.roll(fd, 1, 0))
+        tvg[p] = TV_GAIN * ((left - fa) + (over - fd))
 
     xtab_in.wait()
     for g in range(GROUPS):
-        wait_all(r.at[g], b_recv.at[g])
-
-        def gather(j, carry):
+
+        def gather(k, carry):
+            j = (row // 4 + 8 - k) % 8
+            wait_bytes(r.at[g, pl.ds(0, 128)], b_recv.at[g, j])
             lanes = pl.ds(pl.multiple_of(j * 128, 128), 128)
             for p in range(2):
                 got = swap_blocks([
-                    r[g, pl.ds(pl.multiple_of((4 * j + i) * 32, 32), 32), p * 128:(p + 1) * 128].astype(F32)
+                    r[g, pl.ds(pl.multiple_of((4 * j + i) * 32, 32), 32), p * 128:(p + 1) * 128]
                     for i in range(4)])
                 for c in range(4):
-                    short = got[c].astype(BF16)
+                    short = got[c]
                     other = pl.ds(pl.multiple_of(N + j * 128, 128), 128)
                     line = slice(c * 32, (c + 1) * 32)
                     cross = slice(128 + c * 32, 128 + (c + 1) * 32)
@@ -358,19 +361,6 @@
             return carry
 
         lax.fori_loop(0, 8, gather, 0)
-
-        if g == GROUPS - 1:
-            wait_all(gl, g_recv.at[0])
-
-            def unpack(j, carry):
-                lanes = pl.ds(pl.multiple_of(j * 128, 128), 128)
-                got = swap_blocks([
-                    gl[pl.ds(pl.multiple_of((4 * j + i) * 16, 16), 16), :].astype(F32) for i in range(4)])
-                for hp in range(4):
-                    acc[hp % 2, hp // 2 * 16:hp // 2 * 16 + 16, lanes] += got[hp]
-                return carry
-
-            lax.fori_loop(0, 8, unpack, 0)
 
         def inverse_x(xt, carry):
             cols = pl.ds(pl.multiple_of(xt * 256, 256), 256)
@@ -389,14 +379,28 @@
                 acc[0, :, cols] = gr
                 acc[1, :, cols] = gi
             else:
-                part_s[xt, 0] = (acc[0, :, cols] + gr).astype(BF16)
-                part_s[xt, 1] = (acc[1, :, cols] + gi).astype(BF16)
-                pltpu.make_async_remote_copy(
-                    part_s.at[xt], part_r.at[xt], p_send.at[xt], p_recv.at[xt],
-                    device_id={"coil": 1 - coil}, device_id_type=pl.DeviceIdType.MESH).start()
+                acc[0, :, cols] += gr
+                acc[1, :, cols] += gi
             return carry
 
         lax.fori_loop(0, 4, inverse_x, 0)
+
+    wait_all(gl, g_recv.at[0])
+
+    def unpack(xt, carry):
+        for k in range(2):
+            j = 2 * xt + k
+            lanes = pl.ds(pl.multiple_of(j * 128, 128), 128)
+            got = swap_blocks([gl[pl.ds(pl.multiple_of((4 * j + i) * 16, 16), 16), :] for i in range(4)])
+            for hp in range(4):
+                p, h = hp % 2, slice(hp // 2 * 16, hp // 2 * 16 + 16)
+                part_s[xt, p, h, k * 128:(k + 1) * 128] = (acc[p, h, lanes] + got[hp].astype(F32)).astype(BF16)
+        pltpu.make_async_remote_copy(
+            part_s.at[xt], part_r.at[xt], p_send.at[xt], p_recv.at[xt],
+            device_id={"coil": 1 - coil}, device_id_type=pl.DeviceIdType.MESH).start()
+        return carry
+
+    lax.fori_loop(0, 4, unpack, 0)
 
     def finish(xt, carry):
         wait_bytes(part_r.at[xt], p_recv.at[xt])
@@ -406,14 +410,13 @@
         pltpu.make_async_remote_copy(
             comb.at[frame, xt], comb.at[frame, xt], c_send.at[xt], c_recv.at[xt],
             device_id={"frame": 1 - frame}, device_id_type=pl.DeviceIdType.MESH).start()
+        pltpu.make_async_copy(comb.at[frame, xt], out_hbm.at[frame, xt], o_sem.at[0, xt]).start()
         return carry
 
     lax.fori_loop(0, 4, finish, 0)
     for xt in range(4):
         wait_bytes(comb.at[1 - frame, xt], c_recv.at[xt])
-        for t in range(2):
-            for p in range(2):
-                out_ref[t, p, :, xt * 256:(xt + 1) * 256] = comb[t, xt, p]
+        pltpu.make_async_copy(comb.at[1 - frame, xt], out_hbm.at[1 - frame, xt], o_sem.at[1, xt]).start()
     for xt in range(4):
         wait_bytes(comb.at[frame, xt], c_send.at[xt])
         wait_bytes(part_s.at[xt], p_send.at[xt])
@@ -421,6 +424,9 @@
     wait_all(fs, f_send.at[0])
     wait_all(gs, g_send.at[0])
     share.wait_send()
+    for k in range(2):
+        for xt in range(4):
+            wait_bytes(comb.at[frame, xt], o_sem.at[k, xt])
     for g in range(GROUPS):
         wait_all(b.at[g], b_send.at[g])
 
@@ -432,7 +438,7 @@
 
 
 def outer_kernel(v_hbm, g_hbm, out_hbm, v_ref, g_ref, first, second, out, in_sem, sem):
-    g_in = [pltpu.make_async_copy(g_hbm.at[:, p], g_ref.at[:, p], in_sem.at[p]) for p in range(2)]
+    g_in = [pltpu.make_async_copy(g_hbm.at[:, :, p], g_ref.at[:, :, p], in_sem.at[p]) for p in range(2)]
     v_in = pltpu.make_async_copy(v_hbm, v_ref, in_sem.at[2])
     v_in.start()
     for copy in g_in:
@@ -447,10 +453,10 @@
 
         def some(block, carry):
             for top in range(0, ROWS, 8):
-                for half in range(0, N, 512):
-                    part = (slice(top, top + 8), slice(half, half + 512))
-                    g0 = g_ref[0, p, part[0], part[1]]
-                    g1 = g_ref[1, p, part[0], part[1]]
+                for half in range(0, N, 256):
+                    part = (slice(top, top + 8), slice(half, half + 256))
+                    g0 = g_ref[0, half // 256, p, part[0], :]
+                    g1 = g_ref[1, half // 256, p, part[0], :]
                     for k in range(step):
                         at = block * step + k
                         out[p, at, part[0], part[1]] = first[pl.ds(at, 1), :] * g0 + second[pl.ds(at, 1), :] * g1
@@ -467,9 +473,9 @@
     dma = pltpu.SemaphoreType.DMA
     combined = pl.pallas_call(
         main_kernel,
-        out_shape=jax.ShapeDtypeStruct((2, 2, ROWS, N), F32),
+        out_shape=jax.ShapeDtypeStruct((2, 4, 2, ROWS, 256), F32),
         in_specs=[anywhere] * 8,
-        out_specs=pl.BlockSpec(memory_space=pltpu.VMEM),
+        out_specs=anywhere,
         scratch_shapes=[
             pltpu.VMEM((2, RANK, ROWS, N), BF16),
             pltpu.VMEM((2, COILS, ROWS, N), BF16),
@@ -505,8 +511,8 @@
             pltpu.VMEM((2, 4, 2, ROWS, 256), F32),
             pltpu.VMEM((2, ROWS, N), F32),
             dma((4,)), dma((7,)), dma((2,)), dma((2,)),
-            dma((1,)), dma((1,)), dma((1,)), dma((1,)), dma((1,)), dma((1,)), dma((GROUPS,)), dma((GROUPS,)),
-            dma((1,)), dma((1,)), dma((4,)), dma((4,)), dma((4,)), dma((4,)),
+            dma((1,)), dma((1,)), dma((1,)), dma((1,)), dma((1,)), dma((1,)), dma((GROUPS,)), dma((GROUPS, 8)),
+            dma((1,)), dma((1,)), dma((4,)), dma((4,)), dma((4,)), dma((4,)), dma((2, 4)),
         ],
         compiler_params=pltpu.CompilerParams(
             collective_id=0, has_side_effects=True, vmem_limit_bytes=VMEM_LIMIT
@@ -520,8 +526,8 @@
         in_specs=[anywhere] * 2,
         out_specs=anywhere,
         scratch_shapes=[
-            pltpu.VMEM((2, RANK), BF16), pltpu.VMEM((2, 2, ROWS, N), F32),
-            pltpu.VMEM((RANK, 512), F32), pltpu.VMEM((RANK, 512), F32),
+            pltpu.VMEM((2, RANK), BF16), pltpu.VMEM((2, 4, 2, ROWS, 256), F32),
+            pltpu.VMEM((RANK, 256), F32), pltpu.VMEM((RANK, 256), F32),
             pltpu.VMEM((2, RANK, ROWS, N), F32), dma((3,)), dma,
         ],
         compiler_params=pltpu.CompilerParams(vmem_limit_bytes=VMEM_LIMIT),

time: 52.7 us -> 47.7 us (0.905)
  Pallas kernels: 52.6 us -> 47.5 us
    pallas_call x1, Pallas kernels: 47 us -> 41.9 us  [shards(): pl.pallas_call(main_kernel, out_shape=jax.ShapeDtypeStruct((2, 4, 2, ROWS...]
where the time goes in v3:
time: 47.7 us; the launch traced here: 47.5 us
  Pallas kernels  47.5 us (100%)
    pallas_call x1, Pallas kernels, shards(): pl.pallas_call(main_kernel, out_shape=jax.ShapeDtypeStruct((2, 4, 2, ROWS...  41.9 us
    pallas_call x1, Pallas kernels, shards(): pl.pallas_call(outer_kernel, out_shape=jax.ShapeDtypeStruct((2, RANK, ROW...  5.6 us

profile of v3, /device:TPU:1, one launch (start us, length us, event | category | flops | bytes accessed | tf_op | source)
XLA Modules:
  0.0 47.5 jit_solution(16029675536476276572)
XLA Ops:
  0.0 41.9 %frame_gradient.1.g_hbm = f32[2,4,2,32,256]{4,3,2,1,0:T(8,128)} custom-call(bf16[2,48]{1,0:T(2,128)(2,1)} %v_hbm.3, s32[1,1024]{1,0:T(1,128)} %mask_hbm.1, bf16[2,48,32,1024]{3,2,1,0:T(8,128)(2,1)} %u_hbm.1, bf16[2,8,32,1024]{3,2,1,0:T(8,128)(2,1)} %s_hbm.1, bf16[2,1,8,32,1024]{4,3,2,1,0:T(8,128)(2,1)} %d_hbm.1, f32[32,1024]{1,0:T(8,128)} %w_hbm.1, ...), custom_call_target="tpu_custom_call" | custom-call | flops 6000000000 | bytes 14000000 | tf_op jit(solution)/shard_map/frame_gradient/pallas_call | solution.py:474
  41.9 5.6 %spread_over_rank.1 = f32[2,48,32,1024]{3,2,1,0:T(8,128)} custom-call(bf16[2,48]{1,0:T(2,128)(2,1)} %v_hbm.3, f32[2,4,2,32,256]{4,3,2,1,0:T(8,128)} %frame_gradient.1.g_hbm), custom_call_target="tpu_custom_call" | custom-call | flops 10000000 | bytes 13000000 | tf_op jit(solution)/shard_map/spread_over_rank/pallas_call | solution.py:523

commit v4 on v3

--- a/solution.py
+++ b/solution.py
@@ -124,7 +124,7 @@
                 x[pl.ds(pl.multiple_of((j * 4 + i) * 32, 32), 32), p * 128:(p + 1) * 128] = w4[i]
         return carry
 
-    lax.fori_loop(0, 8, lay_maps, 0)
+    lax.fori_loop(0, 8, lay_maps, 0, unroll=8)
     pl.semaphore_wait(barrier, DEVS + 1)
     send_all(x, land.at[frame], s_send.at[0], s_recv.at[0], 32)
 
@@ -148,7 +148,7 @@
             fs[pl.ds(pl.multiple_of(to * 16, 16), 16), :] = w4[i].astype(BF16)
         return carry
 
-    lax.fori_loop(0, 8, send_frame, 0)
+    lax.fori_loop(0, 8, send_frame, 0, unroll=4)
     send_all(fs, fl, f_send.at[0], f_recv.at[0], 16)
 
     w_in.wait()
@@ -198,7 +198,7 @@
                 b[g, pl.ds(pl.multiple_of(p * 256 + turn * 32, 32), 32), :] = value.astype(BF16)
             return inner
 
-        lax.fori_loop(0, 8, back, 0)
+        lax.fori_loop(0, 8, back, 0, unroll=2)
         return carry
 
     def send_measured(g):
@@ -268,7 +268,7 @@
                 uq[q, pl.ds(256 + at, 32), 128:] = -real
             return inner
 
-        lax.fori_loop(0, 8, spread, 0)
+        lax.fori_loop(0, 8, spread, 0, unroll=2)
         for q in range(4):
             spectrum = dot(ytab[0, q], uq[q])
             keep = mcol[q]
@@ -306,7 +306,7 @@
                     gs[pl.ds(pl.multiple_of(to * 16, 16), 16), :] = jnp.where(block < 2, upper, lower).astype(BF16)
             return inner
 
-        lax.fori_loop(0, 8, collect, 0)
+        lax.fori_loop(0, 8, collect, 0, unroll=2)
     send_all(gs, gl, g_send.at[0], g_recv.at[0], 16)
 
     up.wait()
@@ -339,9 +339,10 @@
     xtab_in.wait()
     for g in range(GROUPS):
 
-        def gather(k, carry):
-            j = (row // 4 + 8 - k) % 8
+        for j in range(8):
             wait_bytes(r.at[g, pl.ds(0, 128)], b_recv.at[g, j])
+
+        def gather(j, carry):
             lanes = pl.ds(pl.multiple_of(j * 128, 128), 128)
             for p in range(2):
                 got = swap_blocks([
@@ -360,7 +361,19 @@
                         lmat[cross, lanes] = short
             return carry
 
-        lax.fori_loop(0, 8, gather, 0)
+        lax.fori_loop(0, 8, gather, 0, unroll=8)
+
+        if g == GROUPS - 1:
+            wait_all(gl, g_recv.at[0])
+
+            def unpack(j, carry):
+                lanes = pl.ds(pl.multiple_of(j * 128, 128), 128)
+                got = swap_blocks([gl[pl.ds(pl.multiple_of((4 * j + i) * 16, 16), 16), :] for i in range(4)])
+                for hp in range(4):
+                    acc[hp % 2, hp // 2 * 16:hp // 2 * 16 + 16, lanes] += got[hp].astype(F32)
+                return carry
+
+            lax.fori_loop(0, 8, unpack, 0, unroll=8)
 
         def inverse_x(xt, carry):
             cols = pl.ds(pl.multiple_of(xt * 256, 256), 256)
@@ -379,28 +392,14 @@
                 acc[0, :, cols] = gr
                 acc[1, :, cols] = gi
             else:
-                acc[0, :, cols] += gr
-                acc[1, :, cols] += gi
+                part_s[xt, 0] = (acc[0, :, cols] + gr).astype(BF16)
+                part_s[xt, 1] = (acc[1, :, cols] + gi).astype(BF16)
+                pltpu.make_async_remote_copy(
+                    part_s.at[xt], part_r.at[xt], p_send.at[xt], p_recv.at[xt],
+                    device_id={"coil": 1 - coil}, device_id_type=pl.DeviceIdType.MESH).start()
             return carry
 
         lax.fori_loop(0, 4, inverse_x, 0)
-
-    wait_all(gl, g_recv.at[0])
-
-    def unpack(xt, carry):
-        for k in range(2):
-            j = 2 * xt + k
-            lanes = pl.ds(pl.multiple_of(j * 128, 128), 128)
-            got = swap_blocks([gl[pl.ds(pl.multiple_of((4 * j + i) * 16, 16), 16), :] for i in range(4)])
-            for hp in range(4):
-                p, h = hp % 2, slice(hp // 2 * 16, hp // 2 * 16 + 16)
-                part_s[xt, p, h, k * 128:(k + 1) * 128] = (acc[p, h, lanes] + got[hp].astype(F32)).astype(BF16)
-        pltpu.make_async_remote_copy(
-            part_s.at[xt], part_r.at[xt], p_send.at[xt], p_recv.at[xt],
-            device_id={"coil": 1 - coil}, device_id_type=pl.DeviceIdType.MESH).start()
-        return carry
-
-    lax.fori_loop(0, 4, unpack, 0)
 
     def finish(xt, carry):
         wait_bytes(part_r.at[xt], p_recv.at[xt])

time: 47.7 us -> 46.5 us (0.975)
  Pallas kernels: 47.5 us -> 46.4 us
    pallas_call x1, Pallas kernels: 41.9 us -> 40.8 us  [shards(): pl.pallas_call(main_kernel, out_shape=jax.ShapeDtypeStruct((2, 4, 2, ROWS...]
where the time goes in v4:
time: 46.5 us; the launch traced here: 46.4 us
  Pallas kernels  46.4 us (100%)
    pallas_call x1, Pallas kernels, shards(): pl.pallas_call(main_kernel, out_shape=jax.ShapeDtypeStruct((2, 4, 2, ROWS...  40.8 us
    pallas_call x1, Pallas kernels, shards(): pl.pallas_call(outer_kernel, out_shape=jax.ShapeDtypeStruct((2, RANK, ROW...  5.6 us

profile of v4, /device:TPU:1, one launch (start us, length us, event | category | flops | bytes accessed | tf_op | source)
XLA Modules:
  0.0 46.4 jit_solution(13717543470318360808)
XLA Ops:
  0.0 40.8 %frame_gradient.1.g_hbm = f32[2,4,2,32,256]{4,3,2,1,0:T(8,128)} custom-call(bf16[2,48]{1,0:T(2,128)(2,1)} %v_hbm.3, s32[1,1024]{1,0:T(1,128)} %mask_hbm.1, bf16[2,48,32,1024]{3,2,1,0:T(8,128)(2,1)} %u_hbm.1, bf16[2,8,32,1024]{3,2,1,0:T(8,128)(2,1)} %s_hbm.1, bf16[2,1,8,32,1024]{4,3,2,1,0:T(8,128)(2,1)} %d_hbm.1, f32[32,1024]{1,0:T(8,128)} %w_hbm.1, ...), custom_call_target="tpu_custom_call" | custom-call | flops 6000000000 | bytes 14000000 | tf_op jit(solution)/shard_map/frame_gradient/pallas_call | solution.py:473
  40.8 5.6 %spread_over_rank.1 = f32[2,48,32,1024]{3,2,1,0:T(8,128)} custom-call(bf16[2,48]{1,0:T(2,128)(2,1)} %v_hbm.3, f32[2,4,2,32,256]{4,3,2,1,0:T(8,128)} %frame_gradient.1.g_hbm), custom_call_target="tpu_custom_call" | custom-call | flops 10000000 | bytes 13000000 | tf_op jit(solution)/shard_map/spread_over_rank/pallas_call | solution.py:522

commit v5 on v4

--- a/solution.py
+++ b/solution.py
@@ -306,8 +306,23 @@
                     gs[pl.ds(pl.multiple_of(to * 16, 16), 16), :] = jnp.where(block < 2, upper, lower).astype(BF16)
             return inner
 
-        lax.fori_loop(0, 8, collect, 0, unroll=2)
-    send_all(gs, gl, g_send.at[0], g_recv.at[0], 16)
+        for part in range(2):
+            lax.fori_loop(4 * part, 4 * part + 4, collect, 0, unroll=2)
+            if turn_g == 1:
+                def send_image(k, inner):
+                    to = (k + row // 8) % 4 * 8 + 4 * part + k // 4
+                    mine = pl.ds(pl.multiple_of(row * 16, 16), 16)
+
+                    @pl.when(to != row)
+                    def _():
+                        pltpu.make_async_remote_copy(
+                            gs.at[pl.ds(pl.multiple_of(to * 16, 16), 16)], gl.at[mine], g_send.at[0], g_recv.at[0],
+                            device_id={"row": to}, device_id_type=pl.DeviceIdType.MESH).start()
+                    return inner
+
+                lax.fori_loop(0, 16, send_image, 0)
+    own_rows = pl.ds(pl.multiple_of(row * 16, 16), 16)
+    gl[own_rows, :] = gs[own_rows, :]
 
     up.wait()
     down.wait()
@@ -446,7 +461,7 @@
     values = v_ref[...].astype(F32)
     spread_column(values, 0, first)
     spread_column(values, 1, second)
-    step = 4
+    step = 2
     for p in range(2):
         g_in[p].wait()
 

time: 46.5 us -> 46.4 us (level)
  no operation moved by 1% of the time
where the time goes in v5:
time: 46.4 us; the launch traced here: 46.3 us
  Pallas kernels  46.3 us (100%)
    pallas_call x1, Pallas kernels, shards(): pl.pallas_call(main_kernel, out_shape=jax.ShapeDtypeStruct((2, 4, 2, ROWS...  40.8 us
    pallas_call x1, Pallas kernels, shards(): pl.pallas_call(outer_kernel, out_shape=jax.ShapeDtypeStruct((2, RANK, ROW...  5.54 us

profile of v5, /device:TPU:1, one launch (start us, length us, event | category | flops | bytes accessed | tf_op | source)
XLA Modules:
  0.0 46.3 jit_solution(16883391887049901538)
XLA Ops:
  0.0 40.8 %frame_gradient.1.g_hbm = f32[2,4,2,32,256]{4,3,2,1,0:T(8,128)} custom-call(bf16[2,48]{1,0:T(2,128)(2,1)} %v_hbm.3, s32[1,1024]{1,0:T(1,128)} %mask_hbm.1, bf16[2,48,32,1024]{3,2,1,0:T(8,128)(2,1)} %u_hbm.1, bf16[2,8,32,1024]{3,2,1,0:T(8,128)(2,1)} %s_hbm.1, bf16[2,1,8,32,1024]{4,3,2,1,0:T(8,128)(2,1)} %d_hbm.1, f32[32,1024]{1,0:T(8,128)} %w_hbm.1, ...), custom_call_target="tpu_custom_call" | custom-call | flops 6000000000 | bytes 14000000 | tf_op jit(solution)/shard_map/frame_gradient/pallas_call | solution.py:488
  40.8 5.5 %spread_over_rank.1 = f32[2,48,32,1024]{3,2,1,0:T(8,128)} custom-call(bf16[2,48]{1,0:T(2,128)(2,1)} %v_hbm.3, f32[2,4,2,32,256]{4,3,2,1,0:T(8,128)} %frame_gradient.1.g_hbm), custom_call_target="tpu_custom_call" | custom-call | flops 10000000 | bytes 13000000 | tf_op jit(solution)/shard_map/spread_over_rank/pallas_call | solution.py:537
